TPU v7x, 128 devices: a whole 4x4x4 slice. The times are simulated.
128 devices in a mesh: lat: 64 (over z, y, x), lev: 2 (over core).
Axes of the slice: x: 4, y: 4, z: 4, core: 2. Of those that a mesh axis runs over, the one named last changes fastest.
Arguments:
- grid_values: bfloat16 [2560, 64, 5136], P('lat', 'lev'), may hold values from -6 to 6
- lat_counts: int32 [1280], P('lat'), may hold values from 8 to 5136, as said below
- wave_table: int32 [128], replicated, may hold values from 0 to 1279, as said below
- inverses: float32 [2560, 2, 32, 32], P('lat'), may hold values from -1 to 1
- legendre: bfloat16 [128, 2, 640, 1280], P('lat', None, 'lev')
Outputs:
- spectral: bfloat16 [128, 2, 640, 128], P('lat', None, 'lev')
Inputs may be any that keep to these rules, and one draw needn't show every extreme that they name: `lat_counts`: a multiple of 4 on every pair; 8 on the polar pair, 5136 on the pair nearest the equator, 20 + 4 p less 0 to 12 on pair p between. `wave_table`: distinct wavenumbers; 0 and 1279 are always among them.
All inputs are finite; a program needn't handle non-finite values.
Results may differ from a plain program's by a relative error of at most 0.015.
Values may be sent and summed in bfloat16 or wider, within the bound.
No kernel may reach another device: no remote copies, remote signals or barrier semaphores. Data moves between devices by JAX's collectives and lax.ppermute only.
A program may use at most 128 MiB of HBM per device.

v0:
```python
import math

import jax
import jax.numpy as jnp
from jax import lax
from jax.sharding import PartitionSpec as P

TRUNC = 1279


def fourier_table(point_count, wavenumbers, width):
    positions = jnp.arange(width, dtype=jnp.int32)
    phase_index = positions[:, None] * wavenumbers[None, :] % point_count
    angles = phase_index.astype(jnp.float32) * (2.0 * math.pi) / point_count.astype(jnp.float32)
    inside = (positions < point_count)[:, None]
    cosines = jnp.where(inside, jnp.cos(angles), 0.0)
    sines = jnp.where(inside, -jnp.sin(angles), 0.0)
    return jnp.concatenate([cosines, sines], axis=1).astype(jnp.bfloat16)


def mix_levels(fourier, inverses):
    band = fourier.shape[0]
    fields = inverses.shape[1]
    levels = inverses.shape[2]
    slots = fourier.shape[3]
    split_data = fourier.astype(jnp.float32).reshape(band, levels, fields, 2, slots)
    mixed = jnp.einsum("aflk,akfrs->sarlf", inverses, split_data, precision=lax.Precision.HIGHEST)
    return mixed.reshape(slots, band, 2, levels * fields)


def fold_pairs(owned):
    wave_count = owned.shape[0]
    all_lats = owned.shape[1]
    columns = owned.shape[3]
    paired = owned.reshape(wave_count, all_lats // 2, 2, 2 * columns)
    return jnp.stack(
        [paired[:, :, 0] + paired[:, :, 1], paired[:, :, 0] - paired[:, :, 1]], axis=1
    ).astype(jnp.bfloat16)


def on_device(grid_values, lat_counts, wave_table, inverses, legendre):
    pair_total = lat_counts.shape[0]
    slab_width = grid_values.shape[1]
    slot_total = wave_table.shape[0]
    storage = grid_values.shape[2]
    grouped = grid_values.reshape(pair_total, 2 * slab_width, storage)

    def transform(item):
        pair_rows, point_count = item
        basis = fourier_table(point_count, wave_table, storage)
        product = jnp.dot(pair_rows, basis, preferred_element_type=jnp.float32)
        product = product / point_count.astype(jnp.float32)
        return product.astype(jnp.bfloat16).reshape(2, slab_width, 2, slot_total)

    fourier = lax.map(transform, (grouped, lat_counts)).reshape(
        2 * pair_total, slab_width, 2, slot_total
    )
    every_level = lax.all_gather(fourier, "lev", axis=1, tiled=True)
    mixed_band = mix_levels(every_level, inverses)
    own_slab = lax.dynamic_slice_in_dim(
        mixed_band, lax.axis_index("lev") * slab_width, slab_width, 3
    )
    slab_owned = lax.all_to_all(
        own_slab.astype(jnp.bfloat16), "lat", split_axis=0, concat_axis=1, tiled=True
    ).astype(own_slab.dtype)
    owned = lax.all_gather(slab_owned.astype(jnp.bfloat16), "lev", axis=3, tiled=True).astype(
        slab_owned.dtype
    )
    folded = fold_pairs(owned)
    wave_count = folded.shape[0]
    summed = jnp.einsum("wqjp,wqpe->wqje", legendre, folded, preferred_element_type=jnp.float32)
    degree_rows = legendre.shape[2]
    wavenumbers = lax.dynamic_slice_in_dim(
        wave_table, lax.axis_index("lat") * wave_count, wave_count
    )
    steps_index = lax.axis_index("lev") * degree_rows + jnp.arange(degree_rows, dtype=jnp.int32)
    parity = jnp.arange(2, dtype=jnp.int32)
    degree = wavenumbers[:, None, None] + 2 * steps_index[None, None, :] + parity[None, :, None]
    keep = (degree <= TRUNC)[:, :, :, None]
    return jnp.where(keep, summed, 0.0).astype(jnp.bfloat16)


def solution(mesh):
    placed = (
        P("lat", "lev", None),
        P("lat"),
        P(),
        P("lat", None, None, None),
        P("lat", None, "lev", None),
    )
    return jax.shard_map(
        on_device,
        mesh=mesh,
        in_specs=placed,
        out_specs=P("lat", None, "lev", None),
        check_vma=False,
    )
```

profile of v0, /device:TPU:1, one launch (start us, length us, event | category | flops | bytes accessed | tf_op | source)
XLA Modules:
  0.0 989.2 jit_solution(5237779508937216669)
XLA Ops:
  6.5 875.8 %while.10 = (s32[]{:T(128)}, bf16[20,2,32,2,128]{4,1,0,3,2:T(2,128)(2,1)}, bf16[20,64,5136]{2,1,0:T(8,128)(2,1)}, s32[20]{0:T(128)}, s32[128]{0:T(128)}, /*index=5*/s32[]{:T(128)}, s32[]{:T(128)}) while((s32[]{:T(128)}, bf16[20,2,32,2,128]{4,1,0,3,2:T(2,128)(2,1)}, bf16[20,64,5136]{2,1,0:T(8,128)(2,1)}, s32[20]{0:T(128)}, s32[128]{0:T(128)}, ...), condition=%wide.region_1.2_spmd, body=%wide.region_0.1_spmd.sunk | while | flops 184112144 | bytes 6106801 | solution.py:55
  10.5 37.6 %select_convert_fusion.3 = (bf16[5136,128]{1,0:T(8,128)(2,1)S(1)}, bf16[5136,128]{1,0:T(8,128)(2,1)S(1)}) fusion(pred[5136]{0:T(1024)(128)(4,1)S(1)} %iota_compare_fusion.2, f32[]{:T(128)S(6)} %convert_element_type.47, pred[]{:T(512)S(6)} %lt.50, s32[]{:T(128)S(6)} %select_n.53, s32[128]{0:T(128)} %get-tuple-element.102), kind=kLoop, calls=%fused_computation.9.clone.1 | loop fusion | flops 10518528 | bytes 2635289 | tf_op jit(solution)/shard_map/convert
  54.3 37.6 %select_convert_fusion.3 = (bf16[5136,128]{1,0:T(8,128)(2,1)S(1)}, bf16[5136,128]{1,0:T(8,128)(2,1)S(1)}) fusion(pred[5136]{0:T(1024)(128)(4,1)S(1)} %iota_compare_fusion.2, f32[]{:T(128)S(6)} %convert_element_type.47, pred[]{:T(512)S(6)} %lt.50, s32[]{:T(128)S(6)} %select_n.53, s32[128]{0:T(128)} %get-tuple-element.102), kind=kLoop, calls=%fused_computation.9.clone.1 | loop fusion | flops 10518528 | bytes 2635289 | tf_op jit(solution)/shard_map/convert
  98.1 37.6 %select_convert_fusion.3 = (bf16[5136,128]{1,0:T(8,128)(2,1)S(1)}, bf16[5136,128]{1,0:T(8,128)(2,1)S(1)}) fusion(pred[5136]{0:T(1024)(128)(4,1)S(1)} %iota_compare_fusion.2, f32[]{:T(128)S(6)} %convert_element_type.47, pred[]{:T(512)S(6)} %lt.50, s32[]{:T(128)S(6)} %select_n.53, s32[128]{0:T(128)} %get-tuple-element.102), kind=kLoop, calls=%fused_computation.9.clone.1 | loop fusion | flops 10518528 | bytes 2635289 | tf_op jit(solution)/shard_map/convert
  141.9 37.6 %select_convert_fusion.3 = (bf16[5136,128]{1,0:T(8,128)(2,1)S(1)}, bf16[5136,128]{1,0:T(8,128)(2,1)S(1)}) fusion(pred[5136]{0:T(1024)(128)(4,1)S(1)} %iota_compare_fusion.2, f32[]{:T(128)S(6)} %convert_element_type.47, pred[]{:T(512)S(6)} %lt.50, s32[]{:T(128)S(6)} %select_n.53, s32[128]{0:T(128)} %get-tuple-element.102), kind=kLoop, calls=%fused_computation.9.clone.1 | loop fusion | flops 10518528 | bytes 2635289 | tf_op jit(solution)/shard_map/convert
  185.6 37.6 %select_convert_fusion.3 = (bf16[5136,128]{1,0:T(8,128)(2,1)S(1)}, bf16[5136,128]{1,0:T(8,128)(2,1)S(1)}) fusion(pred[5136]{0:T(1024)(128)(4,1)S(1)} %iota_compare_fusion.2, f32[]{:T(128)S(6)} %convert_element_type.47, pred[]{:T(512)S(6)} %lt.50, s32[]{:T(128)S(6)} %select_n.53, s32[128]{0:T(128)} %get-tuple-element.102), kind=kLoop, calls=%fused_computation.9.clone.1 | loop fusion | flops 10518528 | bytes 2635289 | tf_op jit(solution)/shard_map/convert
  229.4 37.6 %select_convert_fusion.3 = (bf16[5136,128]{1,0:T(8,128)(2,1)S(1)}, bf16[5136,128]{1,0:T(8,128)(2,1)S(1)}) fusion(pred[5136]{0:T(1024)(128)(4,1)S(1)} %iota_compare_fusion.2, f32[]{:T(128)S(6)} %convert_element_type.47, pred[]{:T(512)S(6)} %lt.50, s32[]{:T(128)S(6)} %select_n.53, s32[128]{0:T(128)} %get-tuple-element.102), kind=kLoop, calls=%fused_computation.9.clone.1 | loop fusion | flops 10518528 | bytes 2635289 | tf_op jit(solution)/shard_map/convert
  273.2 37.6 %select_convert_fusion.3 = (bf16[5136,128]{1,0:T(8,128)(2,1)S(1)}, bf16[5136,128]{1,0:T(8,128)(2,1)S(1)}) fusion(pred[5136]{0:T(1024)(128)(4,1)S(1)} %iota_compare_fusion.2, f32[]{:T(128)S(6)} %convert_element_type.47, pred[]{:T(512)S(6)} %lt.50, s32[]{:T(128)S(6)} %select_n.53, s32[128]{0:T(128)} %get-tuple-element.102), kind=kLoop, calls=%fused_computation.9.clone.1 | loop fusion | flops 10518528 | bytes 2635289 | tf_op jit(solution)/shard_map/convert
  317.0 37.6 %select_convert_fusion.3 = (bf16[5136,128]{1,0:T(8,128)(2,1)S(1)}, bf16[5136,128]{1,0:T(8,128)(2,1)S(1)}) fusion(pred[5136]{0:T(1024)(128)(4,1)S(1)} %iota_compare_fusion.2, f32[]{:T(128)S(6)} %convert_element_type.47, pred[]{:T(512)S(6)} %lt.50, s32[]{:T(128)S(6)} %select_n.53, s32[128]{0:T(128)} %get-tuple-element.102), kind=kLoop, calls=%fused_computation.9.clone.1 | loop fusion | flops 10518528 | bytes 2635289 | tf_op jit(solution)/shard_map/convert
  360.7 37.6 %select_convert_fusion.3 = (bf16[5136,128]{1,0:T(8,128)(2,1)S(1)}, bf16[5136,128]{1,0:T(8,128)(2,1)S(1)}) fusion(pred[5136]{0:T(1024)(128)(4,1)S(1)} %iota_compare_fusion.2, f32[]{:T(128)S(6)} %convert_element_type.47, pred[]{:T(512)S(6)} %lt.50, s32[]{:T(128)S(6)} %select_n.53, s32[128]{0:T(128)} %get-tuple-element.102), kind=kLoop, calls=%fused_computation.9.clone.1 | loop fusion | flops 10518528 | bytes 2635289 | tf_op jit(solution)/shard_map/convert
  404.5 37.6 %select_convert_fusion.3 = (bf16[5136,128]{1,0:T(8,128)(2,1)S(1)}, bf16[5136,128]{1,0:T(8,128)(2,1)S(1)}) fusion(pred[5136]{0:T(1024)(128)(4,1)S(1)} %iota_compare_fusion.2, f32[]{:T(128)S(6)} %convert_element_type.47, pred[]{:T(512)S(6)} %lt.50, s32[]{:T(128)S(6)} %select_n.53, s32[128]{0:T(128)} %get-tuple-element.102), kind=kLoop, calls=%fused_computation.9.clone.1 | loop fusion | flops 10518528 | bytes 2635289 | tf_op jit(solution)/shard_map/convert
  448.3 37.6 %select_convert_fusion.3 = (bf16[5136,128]{1,0:T(8,128)(2,1)S(1)}, bf16[5136,128]{1,0:T(8,128)(2,1)S(1)}) fusion(pred[5136]{0:T(1024)(128)(4,1)S(1)} %iota_compare_fusion.2, f32[]{:T(128)S(6)} %convert_element_type.47, pred[]{:T(512)S(6)} %lt.50, s32[]{:T(128)S(6)} %select_n.53, s32[128]{0:T(128)} %get-tuple-element.102), kind=kLoop, calls=%fused_computation.9.clone.1 | loop fusion | flops 10518528 | bytes 2635289 | tf_op jit(solution)/shard_map/convert
  492.1 37.6 %select_convert_fusion.3 = (bf16[5136,128]{1,0:T(8,128)(2,1)S(1)}, bf16[5136,128]{1,0:T(8,128)(2,1)S(1)}) fusion(pred[5136]{0:T(1024)(128)(4,1)S(1)} %iota_compare_fusion.2, f32[]{:T(128)S(6)} %convert_element_type.47, pred[]{:T(512)S(6)} %lt.50, s32[]{:T(128)S(6)} %select_n.53, s32[128]{0:T(128)} %get-tuple-element.102), kind=kLoop, calls=%fused_computation.9.clone.1 | loop fusion | flops 10518528 | bytes 2635289 | tf_op jit(solution)/shard_map/convert
  535.9 37.6 %select_convert_fusion.3 = (bf16[5136,128]{1,0:T(8,128)(2,1)S(1)}, bf16[5136,128]{1,0:T(8,128)(2,1)S(1)}) fusion(pred[5136]{0:T(1024)(128)(4,1)S(1)} %iota_compare_fusion.2, f32[]{:T(128)S(6)} %convert_element_type.47, pred[]{:T(512)S(6)} %lt.50, s32[]{:T(128)S(6)} %select_n.53, s32[128]{0:T(128)} %get-tuple-element.102), kind=kLoop, calls=%fused_computation.9.clone.1 | loop fusion | flops 10518528 | bytes 2635289 | tf_op jit(solution)/shard_map/convert
  579.7 37.6 %select_convert_fusion.3 = (bf16[5136,128]{1,0:T(8,128)(2,1)S(1)}, bf16[5136,128]{1,0:T(8,128)(2,1)S(1)}) fusion(pred[5136]{0:T(1024)(128)(4,1)S(1)} %iota_compare_fusion.2, f32[]{:T(128)S(6)} %convert_element_type.47, pred[]{:T(512)S(6)} %lt.50, s32[]{:T(128)S(6)} %select_n.53, s32[128]{0:T(128)} %get-tuple-element.102), kind=kLoop, calls=%fused_computation.9.clone.1 | loop fusion | flops 10518528 | bytes 2635289 | tf_op jit(solution)/shard_map/convert
  623.5 37.6 %select_convert_fusion.3 = (bf16[5136,128]{1,0:T(8,128)(2,1)S(1)}, bf16[5136,128]{1,0:T(8,128)(2,1)S(1)}) fusion(pred[5136]{0:T(1024)(128)(4,1)S(1)} %iota_compare_fusion.2, f32[]{:T(128)S(6)} %convert_element_type.47, pred[]{:T(512)S(6)} %lt.50, s32[]{:T(128)S(6)} %select_n.53, s32[128]{0:T(128)} %get-tuple-element.102), kind=kLoop, calls=%fused_computation.9.clone.1 | loop fusion | flops 10518528 | bytes 2635289 | tf_op jit(solution)/shard_map/convert
  667.3 37.6 %select_convert_fusion.3 = (bf16[5136,128]{1,0:T(8,128)(2,1)S(1)}, bf16[5136,128]{1,0:T(8,128)(2,1)S(1)}) fusion(pred[5136]{0:T(1024)(128)(4,1)S(1)} %iota_compare_fusion.2, f32[]{:T(128)S(6)} %convert_element_type.47, pred[]{:T(512)S(6)} %lt.50, s32[]{:T(128)S(6)} %select_n.53, s32[128]{0:T(128)} %get-tuple-element.102), kind=kLoop, calls=%fused_computation.9.clone.1 | loop fusion | flops 10518528 | bytes 2635289 | tf_op jit(solution)/shard_map/convert
  711.1 37.6 %select_convert_fusion.3 = (bf16[5136,128]{1,0:T(8,128)(2,1)S(1)}, bf16[5136,128]{1,0:T(8,128)(2,1)S(1)}) fusion(pred[5136]{0:T(1024)(128)(4,1)S(1)} %iota_compare_fusion.2, f32[]{:T(128)S(6)} %convert_element_type.47, pred[]{:T(512)S(6)} %lt.50, s32[]{:T(128)S(6)} %select_n.53, s32[128]{0:T(128)} %get-tuple-element.102), kind=kLoop, calls=%fused_computation.9.clone.1 | loop fusion | flops 10518528 | bytes 2635289 | tf_op jit(solution)/shard_map/convert
  754.8 37.6 %select_convert_fusion.3 = (bf16[5136,128]{1,0:T(8,128)(2,1)S(1)}, bf16[5136,128]{1,0:T(8,128)(2,1)S(1)}) fusion(pred[5136]{0:T(1024)(128)(4,1)S(1)} %iota_compare_fusion.2, f32[]{:T(128)S(6)} %convert_element_type.47, pred[]{:T(512)S(6)} %lt.50, s32[]{:T(128)S(6)} %select_n.53, s32[128]{0:T(128)} %get-tuple-element.102), kind=kLoop, calls=%fused_computation.9.clone.1 | loop fusion | flops 10518528 | bytes 2635289 | tf_op jit(solution)/shard_map/convert
  798.6 37.6 %select_convert_fusion.3 = (bf16[5136,128]{1,0:T(8,128)(2,1)S(1)}, bf16[5136,128]{1,0:T(8,128)(2,1)S(1)}) fusion(pred[5136]{0:T(1024)(128)(4,1)S(1)} %iota_compare_fusion.2, f32[]{:T(128)S(6)} %convert_element_type.47, pred[]{:T(512)S(6)} %lt.50, s32[]{:T(128)S(6)} %select_n.53, s32[128]{0:T(128)} %get-tuple-element.102), kind=kLoop, calls=%fused_computation.9.clone.1 | loop fusion | flops 10518528 | bytes 2635289 | tf_op jit(solution)/shard_map/convert
  842.4 37.6 %select_convert_fusion.3 = (bf16[5136,128]{1,0:T(8,128)(2,1)S(1)}, bf16[5136,128]{1,0:T(8,128)(2,1)S(1)}) fusion(pred[5136]{0:T(1024)(128)(4,1)S(1)} %iota_compare_fusion.2, f32[]{:T(128)S(6)} %convert_element_type.47, pred[]{:T(512)S(6)} %lt.50, s32[]{:T(128)S(6)} %select_n.53, s32[128]{0:T(128)} %get-tuple-element.102), kind=kLoop, calls=%fused_computation.9.clone.1 | loop fusion | flops 10518528 | bytes 2635289 | tf_op jit(solution)/shard_map/convert
  885.9 12.4 %all-gather.3.cloned.1.call-done = bf16[40,64,2,128]{3,0,2,1:T(8,128)(2,1)} async-done(((bf16[40,32,2,128]{3,0,2,1:T(8,128)(2,1)}), bf16[40,64,2,128]{3,0,2,1:T(8,128)(2,1)}) %all-gather.3.cloned.1.call-update) | async-done | bytes 1310736 | tf_op jit(solution)/shard_map/all_gather | solution.py:58
  903.3 4.7 copy.31
  908.0 5.7 reshape.111
  913.7 24.2 %all_to_all.18 = bf16[64,2,2560]{2,1,0:T(2,128)(2,1)} all-to-all(bf16[64,2,2560]{2,1,0:T(2,128)(2,1)} %reshape.111), channel_id=1, replica_groups=mesh['lat'=64,'lev'=2] {'lat'}, dimensions={0} | all-to-all | bytes 1310720 | tf_op jit(solution)/shard_map/all_to_all | solution.py:63
  937.9 5.8 reshape.112
  943.7 4.3 copy.32
  948.0 4.7 all_to_all.16
  952.9 9.2 all-gather.5.cloned.1.call-done
  962.0 6.6 copy.33
  968.6 7.3 reshape.109
  975.9 4.4 fusion.38
  (119 shorter events, 96.9 us)
Async XLA Ops:
  6.5 974.0 %copy-start = (bf16[2,2,320,1280]{3,2,1,0:T(8,128)(2,1)S(1)}, bf16[2,2,320,1280]{3,2,1,0:T(8,128)(2,1)}, u32[]{:S(2)}) copy-start(bf16[2,2,320,1280]{3,2,1,0:T(8,128)(2,1)} %param.11) | copy-start | bytes 9830404
  6.5 891.8 %all-gather.3.cloned.1.call-start = ((), (), s32[]{:S(2)}) async-start(), calls=%async_computation.1 | async-start | bytes 1966080 | tf_op jit(solution)/shard_map/all_gather | solution.py:58
  882.4 79.6 %all-gather.5.cloned.1.call-start = ((), (), s32[]{:S(2)}) async-start(), calls=%async_computation.2 | async-start | bytes 1966080 | tf_op jit(solution)/shard_map/all_gather | solution.py:66
  948.0 4.7 copy-start.1
Sparse Core Ops, SparseCore 0:
  882.5 15.7 all-gather.2
  952.8 9.1 all-gather.4
where the time goes:
time: 992 us; the launch traced here: 989 us
  other arithmetic  764 us (77%)
  local copies, waits for them, and re-layouts  88.3 us (9%)
  matrix products  38.9 us (4%)
  loops' own time  38 us (4%)
  blocking collectives  24.2 us (2%)
  waiting for transfers between devices  21.7 us (2%)
  between operations  13.5 us (1%)
    another operation x20, other arithmetic  751 us
    another operation x1, loops' own time, on_device(): lax.map(transform, (grouped, lat_counts))  38 us
    dot_general x20, matrix products, transform(): product = jnp.dot(pair_rows, basis, preferred_element_type=jnp.float32)  34 us
    dynamic_slice x20, local copies, waits for them, and re-layouts, on_device(): lax.map(transform, (grouped, lat_counts))  26.2 us
    all_to_all x1, blocking collectives, on_device(): lax.all_to_all(own_slab.astype(jnp.bfloat16), 'lat', split_axis=0, concat...  24.2 us
  transfers between devices with their start and end apart: 2, of which 2 were waited for; matrix products, arithmetic and copies ran while one was open for 0% of the time, Pallas kernels for 0%

commit v1 on v0

v1 whole, which is shorter than its diff:
```python
import functools

import jax
import jax.numpy as jnp
from jax import lax
from jax.experimental import pallas as pl
from jax.experimental.pallas import tpu as pltpu
from jax.sharding import PartitionSpec as P

TRUNC = 1279
BLOCK = 256
PAIRS_PER_STEP = 4
MIX_PAIRS = 5
VMEM_LIMIT = 56 * 2**20

COS_TERMS = (1.0, -19.73920440673828, 64.9391098022461, -85.45005798339844,
             60.16698455810547, -25.965150833129883, 6.525190353393555)
SIN_TERMS = (6.2831854820251465, -41.34170150756836, 81.60513305664062, -76.7029800415039,
             42.02566146850586, -14.898837089538574, 3.236703872680664)

f32 = jnp.float32
bf16 = jnp.bfloat16


def horner(z, terms):
    total = jnp.full_like(z, terms[-1])
    for term in terms[-2::-1]:
        total = total * z + term
    return total


def iota(shape, dim):
    return lax.broadcasted_iota(jnp.int32, shape, dim)


def fourier_kernel(counts, waves, grid, out, wave_row, tail):
    step = pl.program_id(0)
    pairs, rows, storage = grid.shape
    blocks = storage // BLOCK
    rest = storage - blocks * BLOCK

    @pl.when(step == 0)
    def _():
        table = jnp.broadcast_to(waves[...], (8, 128))
        order = (iota((128, 128), 0) == (iota((128, 128), 1) % 64) * 2 + iota((128, 128), 1) // 64)
        order = order.astype(f32).astype(bf16)
        high = jnp.dot((table // 64).astype(f32).astype(bf16), order, preferred_element_type=f32)
        low = jnp.dot((table % 64).astype(f32).astype(bf16), order, preferred_element_type=f32)
        wave_row[...] = high * 64.0 + low
        tail[...] = jnp.zeros_like(tail)

    row = iota((40, 128), 0)
    position = jnp.where(row < 16, row, jnp.where(row < 32, (row - 16) * 16, BLOCK)).astype(f32)
    turns = position * wave_row[0:1, :]
    lane = iota((16, BLOCK), 1)
    for i in range(pairs):
        count = counts[step * pairs + i]
        count_f = jnp.full((8, 128), count, jnp.int32).astype(f32)
        inverse = 1.0 / count_f
        inverse5 = jnp.concatenate([inverse] * 5, 0)
        count5 = jnp.concatenate([count_f] * 5, 0)
        whole = jnp.floor(turns * inverse5 + 0.5)
        u = (turns - whole * count5) * inverse5
        z = u * u
        cosine = horner(z, COS_TERMS)
        sine = u * horner(z, SIN_TERMS)
        cos_fine, sin_fine = cosine[0:16], sine[0:16]
        cos_part, sin_part = [], []
        for a in range(16):
            c, s = cosine[16 + a:17 + a], sine[16 + a:17 + a]
            cos_part.append(c * cos_fine - s * sin_fine)
            sin_part.append(-(s * cos_fine + c * sin_fine))
        basis = jnp.concatenate(
            [jnp.concatenate(cos_part, 0), jnp.concatenate(sin_part, 0)], 1
        ).astype(bf16)
        turn_r, turn_i = cosine[32:33], -sine[32:33]
        tail[i, :, 0:rest] = grid[i, :, blocks * BLOCK:storage]
        pieces = []
        for b in range(blocks + 1):
            piece = grid[i, :, b * BLOCK:(b + 1) * BLOCK] if b < blocks else tail[i]
            inside = jnp.where(lane + b * BLOCK < count, 1.0, 0.0).astype(bf16)
            pieces.append(piece * jnp.concatenate([inside] * (rows // 16), 0))
        product = jnp.dot(jnp.concatenate(pieces, 0), basis, preferred_element_type=f32)
        real = imag = None
        for b in range(blocks, -1, -1):
            new_r = product[b * rows:(b + 1) * rows, :128]
            new_i = product[b * rows:(b + 1) * rows, 128:]
            if real is None:
                real, imag = new_r, new_i
            else:
                real, imag = (
                    real * turn_r - imag * turn_i + new_r,
                    real * turn_i + imag * turn_r + new_i,
                )
        scale = inverse[0:1]
        out[i] = jnp.concatenate([real * scale, imag * scale], 1).astype(bf16)


def fourier(grouped, lat_counts, wave_table):
    pair_total, rows, storage = grouped.shape
    step = PAIRS_PER_STEP
    return pl.pallas_call(
        fourier_kernel,
        out_shape=jax.ShapeDtypeStruct((pair_total, rows, 256), bf16),
        grid=(pair_total // step,),
        in_specs=[
            pl.BlockSpec(memory_space=pltpu.SMEM),
            pl.BlockSpec((1, 128), lambda i: (0, 0)),
            pl.BlockSpec((step, rows, storage), lambda i: (i, 0, 0)),
        ],
        out_specs=pl.BlockSpec((step, rows, 256), lambda i: (i, 0, 0)),
        scratch_shapes=[pltpu.VMEM((8, 128), f32), pltpu.VMEM((step, rows, BLOCK), bf16)],
        compiler_params=pltpu.CompilerParams(vmem_limit_bytes=VMEM_LIMIT),
        name="fourier",
    )(lat_counts, wave_table.reshape(1, 128), grouped)


def mix_kernel(inverses, own, other, out, rows_out):
    step = pl.program_id(0)
    slab = lax.axis_index("lev")
    pairs = own.shape[0]
    spread_level = iota((32, 128), 0)
    spread_lane = iota((32, 128), 1)
    level = (((spread_lane >> 5) & 1) ^ slab) * 16 + ((spread_lane >> 1) & 15)
    spread = (spread_level == level).astype(f32).astype(bf16)
    matrices = jnp.dot(inverses[...], spread, preferred_element_type=f32)
    row = iota(matrices.shape, 0)
    lane = iota(matrices.shape, 1)
    keep = ((row & 1) == (lane & 1)) & (((row >> 5) & 1) == (lane >> 6))
    matrices = jnp.where(keep, matrices, 0.0)
    for i in range(pairs):
        north = matrices[i * 64:i * 64 + 32]
        south = matrices[i * 64 + 32:i * 64 + 64]
        fold = jnp.concatenate([north + south, north - south], 0).astype(bf16)
        values = jnp.concatenate(
            [own[i, 0:32], other[i, 0:32], own[i, 32:64], other[i, 32:64]], 0
        )
        mixed = jnp.dot(fold, values, preferred_element_type=f32)
        stacked = jnp.concatenate(
            [mixed[0:32, :128], mixed[0:32, 128:], mixed[32:64, :128], mixed[32:64, 128:]], 0
        )
        turned = stacked.T
        pair = step * pairs + i
        rows_out[pl.ds(2 * pair, 64, stride=40), :] = turned[0:64]
        rows_out[pl.ds(2 * pair + 1, 64, stride=40), :] = turned[64:128]

    @pl.when(step == pl.num_programs(0) - 1)
    def _():
        out[...] = rows_out[...].astype(bf16)


def mix(inverses, own, other):
    pair_total = own.shape[0]
    step = MIX_PAIRS
    return pl.pallas_call(
        mix_kernel,
        out_shape=jax.ShapeDtypeStruct((2560, 128), bf16),
        grid=(pair_total // step,),
        in_specs=[
            pl.BlockSpec((step * 64, 32), lambda i: (i, 0)),
            pl.BlockSpec((step, 64, 256), lambda i: (i, 0, 0)),
            pl.BlockSpec((step, 64, 256), lambda i: (i, 0, 0)),
        ],
        out_specs=pl.BlockSpec((2560, 128), lambda i: (0, 0)),
        scratch_shapes=[pltpu.VMEM((2560, 128), f32)],
        compiler_params=pltpu.CompilerParams(vmem_limit_bytes=VMEM_LIMIT),
        name="mix",
    )(inverses, own, other)


def legendre_kernel(waves, own, other, table, out, even, odd, folded):
    slot = pl.program_id(0)
    parity = pl.program_id(1)
    slab = lax.axis_index("lev")
    owner = lax.axis_index("lat")
    degree_rows = table.shape[2]

    @pl.when((slot == 0) & (parity == 0))
    def _():
        row = iota((256, 256), 0)
        target = (
            ((row >> 6) & 1) * 128 + ((row >> 5) & 1) * 64 + ((row >> 7) ^ slab) * 32 + (row & 31)
        )
        order = (iota((256, 256), 1) == target).astype(f32).astype(bf16)
        both = jnp.concatenate([own[...], other[...]], 1)
        ordered = jnp.dot(both, order, preferred_element_type=f32)
        even[...] = ordered[:, :128]
        odd[...] = ordered[:, 128:]
        for s in range(2):
            folded[s, 0] = even[pl.ds(s, 1280, stride=2), :].astype(bf16)
            folded[s, 1] = odd[pl.ds(s, 1280, stride=2), :].astype(bf16)

    summed = jnp.dot(table[0, 0], folded[slot, parity], preferred_element_type=f32)
    wave = waves[owner * 2 + slot]
    degree = wave + 2 * (slab * degree_rows + iota(summed.shape, 0)) + parity
    out[0, 0] = jnp.where(degree <= TRUNC, summed, 0.0).astype(bf16)


def legendre_sum(wave_table, own, other, table):
    slots, parities, degree_rows, pairs = table.shape
    return pl.pallas_call(
        legendre_kernel,
        out_shape=jax.ShapeDtypeStruct((slots, parities, degree_rows, 128), bf16),
        grid=(slots, parities),
        in_specs=[
            pl.BlockSpec(memory_space=pltpu.SMEM),
            pl.BlockSpec((2560, 128), lambda s, q: (0, 0)),
            pl.BlockSpec((2560, 128), lambda s, q: (0, 0)),
            pl.BlockSpec((1, 1, degree_rows, pairs), lambda s, q: (s, q, 0, 0)),
        ],
        out_specs=pl.BlockSpec((1, 1, degree_rows, 128), lambda s, q: (s, q, 0, 0)),
        scratch_shapes=[
            pltpu.VMEM((2560, 128), f32),
            pltpu.VMEM((2560, 128), f32),
            pltpu.VMEM((2, 2, 1280, 128), bf16),
        ],
        compiler_params=pltpu.CompilerParams(vmem_limit_bytes=VMEM_LIMIT),
        name="legendre",
    )(wave_table, own, other, table)


def on_device(grid_values, lat_counts, wave_table, inverses, legendre):
    pair_total = lat_counts.shape[0]
    slab_width = grid_values.shape[1]
    grouped = grid_values.reshape(pair_total, 2 * slab_width, grid_values.shape[2])
    swap = [(0, 1), (1, 0)]
    own = fourier(grouped, lat_counts, wave_table)
    other = lax.ppermute(own, "lev", swap)
    half = lax.dynamic_slice_in_dim(inverses, lax.axis_index("lev") * 16, 16, 2)
    half = half.astype(bf16).transpose(0, 2, 1, 3).reshape(2 * pair_total * 32, 32)
    send = mix(half, own, other)
    slab = lax.all_to_all(
        send.reshape(64, 40, 128), "lat", split_axis=0, concat_axis=0, tiled=True
    )
    rest = lax.ppermute(slab, "lev", swap)
    return legendre_sum(wave_table, slab.reshape(2560, 128), rest.reshape(2560, 128), legendre)


def solution(mesh):
    placed = (
        P("lat", "lev", None),
        P("lat"),
        P(),
        P("lat", None, None, None),
        P("lat", None, "lev", None),
    )
    return jax.shard_map(
        on_device,
        mesh=mesh,
        in_specs=placed,
        out_specs=P("lat", None, "lev", None),
        check_vma=False,
    )
```

time: 992 us -> 55.5 us (0.06)
  other arithmetic: 764 us -> 0 us
  local copies, waits for them, and re-layouts: 88.3 us -> 2.93 us
  matrix products: 38.9 us -> 0 us
  loops' own time: 38 us -> 0 us
  Pallas kernels: 0 us -> 21.4 us
  waiting for transfers between devices: 21.7 us -> 2.39 us
  between operations: 13.5 us -> 0.01 us
    another operation x20 -> x0, other arithmetic: 751 us -> none
    dot_general x22 -> x0, matrix products: 38.9 us -> none  [the longest x20 34 us: transform(): product = jnp.dot(pair_rows, basis, preferred_element_type=jnp.float32)]
    another operation x1 -> x0, loops' own time: 38 us -> none  [on_device(): lax.map(transform, (grouped, lat_counts))]
    dynamic_slice x21 -> x0, local copies, waits for them, and re-layouts: 26.2 us -> none  [the longest x20 26.2 us: on_device(): lax.map(transform, (grouped, lat_counts))]
    all_gather x2 -> x0, waiting for transfers between devices: 21.6 us -> none  [the longest x1 12.4 us: on_device(): every_level = lax.all_gather(fourier, 'lev', axis=1, tiled=True)]
    pallas_call x0 -> x3, Pallas kernels: none -> 21.4 us  [the longest x1 11.5 us: fourier(): pl.pallas_call(fourier_kernel, out_shape=jax.ShapeDtypeStruct((pair_total...]
    reshape x2 -> x0, local copies, waits for them, and re-layouts: 13.9 us -> none  [fold_pairs(): paired = owned.reshape(wave_count, all_lats // 2, 2, 2 * columns)]
    dynamic_update_slice x20 -> x0, local copies, waits for them, and re-layouts: 13.3 us -> none  [on_device(): lax.map(transform, (grouped, lat_counts))]
  transfers between devices with their start and end apart: 2 -> 2, of which waited for: 2 -> 2; matrix products, arithmetic and copies ran while one was open for 0% -> 2% of each run, Pallas kernels for 0% -> 0%
where the time goes in v1:
time: 55.5 us; the launch traced here: 55 us
  blocking collectives  25.1 us (45%)
  Pallas kernels  21.4 us (39%)
  starting transfers between devices  3.23 us (6%)
  local copies, waits for them, and re-layouts  2.93 us (5%)
  waiting for transfers between devices  2.39 us (4%)
    all_to_all x1, blocking collectives, on_device(): lax.all_to_all(send.reshape(64, 40, 128), 'lat', split_axis=0, concat_axi...  25.1 us
    pallas_call x1, Pallas kernels, fourier(): pl.pallas_call(fourier_kernel, out_shape=jax.ShapeDtypeStruct((pair_total...  11.5 us
    pallas_call x1, Pallas kernels, legendre_sum(): pl.pallas_call(legendre_kernel, out_shape=jax.ShapeDtypeStruct((slots, pa...  5.54 us
    pallas_call x1, Pallas kernels, mix(): pl.pallas_call(mix_kernel, out_shape=jax.ShapeDtypeStruct((2560, 128), bf...  4.34 us
    ppermute x1, starting transfers between devices, on_device(): rest = lax.ppermute(slab, 'lev', swap)  1.82 us
    ppermute x1, waiting for transfers between devices, on_device(): rest = lax.ppermute(slab, 'lev', swap)  1.72 us
    unnamed x8, local copies, waits for them, and re-layouts  1.66 us
    ppermute x1, starting transfers between devices, on_device(): other = lax.ppermute(own, 'lev', swap)  1.4 us
  transfers between devices with their start and end apart: 2, of which 2 were waited for; matrix products, arithmetic and copies ran while one was open for 2% of the time, Pallas kernels for 0%

profile of v1, /device:TPU:1, one launch (start us, length us, event | category | flops | bytes accessed | tf_op | source)
XLA Modules:
  0.0 55.0 jit_solution(799339233935197353)
XLA Ops:
  0.0 0.0 copy-start
  0.0 11.5 %fourier.1.own = bf16[20,64,256]{2,1,0:T(8,128)(2,1)} custom-call(s32[20]{0:T(128)} %counts.1, s32[1,128]{1,0:T(1,128)} %bitcast.13, bf16[20,64,5136]{2,1,0:T(8,128)(2,1)} %bitcast.8), custom_call_target="tpu_custom_call" | custom-call | tf_op jit(solution)/shard_map/fourier/pallas_call | solution.py:102
  11.5 1.4 %collective-permute-start = (bf16[20,64,256]{2,1,0:T(8,128)(2,1)}, bf16[20,64,256]{2,1,0:T(8,128)(2,1)S(1)}, u32[]{:S(2)}, u32[]{:S(2)}) collective-permute-start(bf16[20,64,256]{2,1,0:T(8,128)(2,1)} %fourier.1.own), channel_id=1, source_target_pairs={{0,1},{1,0},{2,3},{3,2},{4,5},{5,4},{6,7},{7,6},{8,9},{9,8},{10,11... | collective-permute-start | bytes 1966088 | tf_op jit(solution)/shard_map/ppermute | solution.py:228
  12.9 0.0 copy-done
  12.9 1.2 %copy.6 = bf16[40,16,2,32]{3,2,1,0:T(2,128)(2,1)} copy(bf16[40,16,2,32]{0,3,1,2:T(8,128)(2,1)S(1)} %fusion) | data formatting | bytes 163840 | tf_op jit(solution)/shard_map/transpose | solution.py:230
  14.2 0.7 %collective-permute-done.other = bf16[20,64,256]{2,1,0:T(8,128)(2,1)S(1)} collective-permute-done((bf16[20,64,256]{2,1,0:T(8,128)(2,1)}, bf16[20,64,256]{2,1,0:T(8,128)(2,1)S(1)}, u32[]{:S(2)}, u32[]{:S(2)}) %collective-permute-start) | collective-permute-done | bytes 655392 | tf_op jit(solution)/shard_map/ppermute | solution.py:228
  14.8 0.0 copy-start.3
  14.8 0.8 %copy-done.3 = bf16[20,64,256]{2,1,0:T(8,128)(2,1)} copy-done((bf16[20,64,256]{2,1,0:T(8,128)(2,1)}, bf16[20,64,256]{2,1,0:T(8,128)(2,1)S(1)}, u32[]{:S(2)}) %copy-start.3) | copy-done | bytes 655384
  15.7 4.3 %mix.1 = bf16[2560,128]{1,0:T(8,128)(2,1)} custom-call(bf16[1280,32]{1,0:T(8,128)(2,1)} %bitcast.11, bf16[20,64,256]{2,1,0:T(8,128)(2,1)} %fourier.1.own, bf16[20,64,256]{2,1,0:T(8,128)(2,1)} %copy-done.3), custom_call_target="tpu_custom_call" | custom-call | tf_op jit(solution)/shard_map/mix/pallas_call | solution.py:155
  20.0 25.1 %all_to_all.5 = bf16[64,40,128]{2,1,0:T(8,128)(2,1)S(1)} all-to-all(bf16[64,40,128]{2,1,0:T(8,128)(2,1)} %bitcast.10), channel_id=1, replica_groups=mesh['lat'=64,'lev'=2] {'lat'}, dimensions={0} | all-to-all | bytes 1310720 | tf_op jit(solution)/shard_map/all_to_all | solution.py:232
  45.1 0.0 copy-start.1
  45.1 1.8 %collective-permute-start.1 = (bf16[64,40,128]{2,1,0:T(8,128)(2,1)S(1)}, bf16[64,40,128]{2,1,0:T(8,128)(2,1)S(1)}, u32[]{:S(2)}, u32[]{:S(2)}) collective-permute-start(bf16[64,40,128]{2,1,0:T(8,128)(2,1)S(1)} %all_to_all.5), channel_id=1, source_target_pairs={{0,1},{1,0},{2,3},{3,2},{4,5},{5,4},{6,7},{7,6},{8,9},{9,8},{10,11... | collective-permute-start | bytes 1966088 | tf_op jit(solution)/shard_map/ppermute | solution.py:235
  47.0 1.7 %collective-permute-done.1 = bf16[64,40,128]{2,1,0:T(8,128)(2,1)S(1)} collective-permute-done((bf16[64,40,128]{2,1,0:T(8,128)(2,1)S(1)}, bf16[64,40,128]{2,1,0:T(8,128)(2,1)S(1)}, u32[]{:S(2)}, u32[]{:S(2)}) %collective-permute-start.1) | collective-permute-done | bytes 655392 | tf_op jit(solution)/shard_map/ppermute | solution.py:235
  48.7 0.0 copy-start.2
  48.7 0.0 copy-done.1
  48.7 0.8 %copy-done.2 = bf16[64,40,128]{2,1,0:T(8,128)(2,1)} copy-done((bf16[64,40,128]{2,1,0:T(8,128)(2,1)}, bf16[64,40,128]{2,1,0:T(8,128)(2,1)S(1)}, u32[]{:S(2)}) %copy-start.2) | copy-done | bytes 655384
  49.5 5.5 %legendre.1 = bf16[2,2,320,128]{3,2,1,0:T(8,128)(2,1)} custom-call(s32[128]{0:T(128)} %waves.1, bf16[2560,128]{1,0:T(8,128)(2,1)} %bitcast.9, bf16[2560,128]{1,0:T(8,128)(2,1)} %bitcast.12, bf16[2,2,320,1280]{3,2,1,0:T(8,128)(2,1)} %table.1), custom_call_target="tpu_custom_call" | custom-call | tf_op jit(solution)/shard_map/legendre/pallas_call | solution.py:201
  (1 shorter events, 0.0 us)
Async XLA Ops:
  0.0 12.9 %copy-start = (f32[40,2,32,32]{0,3,2,1:T(8,128)S(1)}, f32[40,2,32,32]{0,3,2,1:T(8,128)}, u32[]{:S(2)}) copy-start(f32[40,2,32,32]{0,3,2,1:T(8,128)} %param.8) | copy-start | bytes 983044
  11.5 3.3 %collective-permute-start = (bf16[20,64,256]{2,1,0:T(8,128)(2,1)}, bf16[20,64,256]{2,1,0:T(8,128)(2,1)S(1)}, u32[]{:S(2)}, u32[]{:S(2)}) collective-permute-start(bf16[20,64,256]{2,1,0:T(8,128)(2,1)} %fourier.1.own), channel_id=1, source_target_pairs={{0,1},{1,0},{2,3},{3,2},{4,5},{5,4},{6,7},{7,6},{8,9},{9,8},{10,11... | collective-permute-start | bytes 1966088 | tf_op jit(solution)/shard_map/ppermute | solution.py:228
  14.8 0.8 %copy-start.3 = (bf16[20,64,256]{2,1,0:T(8,128)(2,1)}, bf16[20,64,256]{2,1,0:T(8,128)(2,1)S(1)}, u32[]{:S(2)}) copy-start(bf16[20,64,256]{2,1,0:T(8,128)(2,1)S(1)} %collective-permute-done.other) | copy-start | bytes 1966084
  45.1 3.6 %copy-start.1 = (bf16[64,40,128]{2,1,0:T(8,128)(2,1)}, bf16[64,40,128]{2,1,0:T(8,128)(2,1)S(1)}, u32[]{:S(2)}) copy-start(bf16[64,40,128]{2,1,0:T(8,128)(2,1)S(1)} %all_to_all.5) | copy-start | bytes 1966084
  45.1 3.5 %collective-permute-start.1 = (bf16[64,40,128]{2,1,0:T(8,128)(2,1)S(1)}, bf16[64,40,128]{2,1,0:T(8,128)(2,1)S(1)}, u32[]{:S(2)}, u32[]{:S(2)}) collective-permute-start(bf16[64,40,128]{2,1,0:T(8,128)(2,1)S(1)} %all_to_all.5), channel_id=1, source_target_pairs={{0,1},{1,0},{2,3},{3,2},{4,5},{5,4},{6,7},{7,6},{8,9},{9,8},{10,11... | collective-permute-start | bytes 1966088 | tf_op jit(solution)/shard_map/ppermute | solution.py:235
  48.7 0.8 %copy-start.2 = (bf16[64,40,128]{2,1,0:T(8,128)(2,1)}, bf16[64,40,128]{2,1,0:T(8,128)(2,1)S(1)}, u32[]{:S(2)}) copy-start(bf16[64,40,128]{2,1,0:T(8,128)(2,1)S(1)} %collective-permute-done.1) | copy-start | bytes 1966084

commit v2 on v0

v2 whole, which is shorter than its diff:
```python
import functools

import jax
import jax.numpy as jnp
from jax import lax
from jax.experimental import pallas as pl
from jax.experimental.pallas import tpu as pltpu
from jax.sharding import PartitionSpec as P

TRUNC = 1279
BLOCK = 256
GROUP = 4
AHEAD = 8
MIX_PAIRS = 5
FOURIER_VMEM = 53 * 2**20
MIX_VMEM = 48 * 2**20
LEGENDRE_VMEM = 24 * 2**20

COS_TERMS = (1.0, -19.73920440673828, 64.9391098022461, -85.45005798339844,
             60.16698455810547, -25.965150833129883, 6.525190353393555)
SIN_TERMS = (6.2831854820251465, -41.34170150756836, 81.60513305664062, -76.7029800415039,
             42.02566146850586, -14.898837089538574, 3.236703872680664)

f32 = jnp.float32
bf16 = jnp.bfloat16


def horner(z, terms):
    total = jnp.full_like(z, terms[-1])
    for term in terms[-2::-1]:
        total = total * z + term
    return total


def iota(shape, dim):
    return lax.broadcasted_iota(jnp.int32, shape, dim)


def fourier_kernel(numbers, waves, grid, out, values, bases, turns, tail, sems):
    pairs, rows, storage = grid.shape
    counts = numbers.at[pl.ds(128, pairs)]
    blocks = storage // BLOCK
    rest = storage - blocks * BLOCK

    def fetch(p):
        return pltpu.make_async_copy(grid.at[p], values.at[p], sems.at[p])

    for p in range(AHEAD):
        fetch(p).start()

    table = jnp.broadcast_to(waves[:, 0:128], (8, 128))
    order = iota((128, 128), 0) == (iota((128, 128), 1) % 64) * 2 + iota((128, 128), 1) // 64
    order = order.astype(f32).astype(bf16)
    high = jnp.dot((table // 64).astype(f32).astype(bf16), order, preferred_element_type=f32)
    low = jnp.dot((table % 64).astype(f32).astype(bf16), order, preferred_element_type=f32)
    wave_row = (high * 64.0 + low)[0:1]
    tail[...] = jnp.zeros_like(tail)
    row = iota((40, 128), 0)
    position = jnp.where(row < 16, row, jnp.where(row < 32, (row - 16) * 16, BLOCK)).astype(f32)
    angle_index = position * wave_row
    lane = iota((16, BLOCK), 1).astype(f32).astype(bf16)

    def make_basis(p):
        count_f = jnp.full((8, 128), counts[p], jnp.int32).astype(f32)
        inverse = 1.0 / count_f
        inverse5 = jnp.concatenate([inverse] * 5, 0)
        count5 = jnp.concatenate([count_f] * 5, 0)
        whole = jnp.floor(angle_index * inverse5 + 0.5)
        u = (angle_index - whole * count5) * inverse5
        z = u * u
        cosine = horner(z, COS_TERMS)
        sine = u * horner(z, SIN_TERMS)
        cos_fine, sin_fine = cosine[0:16], sine[0:16]
        for a in range(16):
            c, s = cosine[16 + a:17 + a], sine[16 + a:17 + a]
            bases[p, a * 16:(a + 1) * 16, 0:128] = (c * cos_fine - s * sin_fine).astype(bf16)
            bases[p, a * 16:(a + 1) * 16, 128:256] = (-(s * cos_fine + c * sin_fine)).astype(bf16)
        turns[p] = jnp.concatenate([cosine[32:40], -sine[32:40], inverse], 0)

    def clear_beyond(piece, first, count):
        limit = jnp.full((16, BLOCK), jnp.clip(count - first, 0, BLOCK), jnp.int32)
        inside = lane < limit.astype(f32).astype(bf16)
        zero = jnp.zeros((16, BLOCK), bf16)
        return jnp.concatenate(
            [jnp.where(inside, piece[r:r + 16], zero) for r in range(0, rows, 16)], 0
        )

    def transform(p, i):
        count = counts[p]
        tail[i, :, 0:rest] = values[p, :, blocks * BLOCK:storage]
        pieces = [clear_beyond(tail[i], blocks * BLOCK, count)]
        pieces += [values[p, :, b * BLOCK:(b + 1) * BLOCK] for b in range(blocks - 1, -1, -1)]
        product = jnp.dot(jnp.concatenate(pieces, 0), bases[p], preferred_element_type=f32)
        turn_r, turn_i, scale = turns[p, 0:1], turns[p, 8:9], turns[p, 16:17]
        real, imag = product[0:rows, :128], product[0:rows, 128:]
        for b in range(blocks - 1, -1, -1):
            used = jnp.where((b + 1) * BLOCK < count, 1.0, 0.0)
            step_r, step_i = turn_r * used, turn_i * used
            at = (blocks - b) * rows
            new_r, new_i = product[at:at + rows, :128], product[at:at + rows, 128:]
            real, imag = (
                real * step_r - imag * step_i + new_r,
                real * step_i + imag * step_r + new_i,
            )
        out[p] = jnp.concatenate([real * scale, imag * scale], 1).astype(bf16)

    def basis_step(t, carry):
        for i in range(GROUP):
            make_basis(t * GROUP + i)
        return carry

    lax.fori_loop(0, pairs // GROUP, basis_step, 0)

    def group_step(t, carry):
        @pl.when(t * GROUP + AHEAD < pairs)
        def _():
            for i in range(GROUP):
                fetch(t * GROUP + AHEAD + i).start()

        for i in range(GROUP):
            fetch(t * GROUP + i).wait()
        for i in range(GROUP):
            p = t * GROUP + i
            first = jnp.minimum(counts[p] // BLOCK, blocks - 1) * BLOCK
            at = pl.ds(pl.multiple_of(first, BLOCK), BLOCK)
            values[p, :, at] = clear_beyond(values[p, :, at], first, counts[p])
        for i in range(GROUP):
            transform(t * GROUP + i, i)
        return carry

    lax.fori_loop(0, pairs // GROUP, group_step, 0)


def fourier(grouped, lat_counts, wave_table):
    pairs, rows, storage = grouped.shape
    numbers = jnp.pad(jnp.concatenate([wave_table, lat_counts]), (0, 128 - pairs))
    return pl.pallas_call(
        fourier_kernel,
        out_shape=jax.ShapeDtypeStruct((pairs, rows, 256), bf16),
        in_specs=[
            pl.BlockSpec(memory_space=pltpu.SMEM),
            pl.BlockSpec(memory_space=pltpu.VMEM),
            pl.BlockSpec(memory_space=pl.ANY),
        ],
        out_specs=pl.BlockSpec(memory_space=pltpu.VMEM),
        scratch_shapes=[
            pltpu.VMEM((pairs, rows, storage), bf16),
            pltpu.VMEM((pairs, BLOCK, 256), bf16),
            pltpu.VMEM((pairs, 24, 128), f32),
            pltpu.VMEM((GROUP, rows, BLOCK), bf16),
            pltpu.SemaphoreType.DMA((pairs,)),
        ],
        compiler_params=pltpu.CompilerParams(vmem_limit_bytes=FOURIER_VMEM),
        name="fourier",
    )(numbers, numbers.reshape(1, 256), grouped)


def mix_kernel(inverses, own, other, table, out, table_out, rows_out, sem):
    bring = pltpu.make_async_copy(table, table_out, sem)
    bring.start()
    slab = lax.axis_index("lev")
    pairs = own.shape[0]
    lane = iota((32, 128), 1)
    level = (((lane >> 5) & 1) ^ slab) * 16 + ((lane >> 1) & 15)
    spread = (iota((32, 128), 0) == level).astype(f32).astype(bf16)
    row = iota((64 * MIX_PAIRS, 128), 0)
    lane = iota((64 * MIX_PAIRS, 128), 1)
    keep = ((row & 1) == (lane & 1)) & (((row >> 5) & 1) == (lane >> 6))

    def group_step(t, carry):
        first = pl.multiple_of(t * 64 * MIX_PAIRS, 64 * MIX_PAIRS)
        matrices = jnp.dot(
            inverses[pl.ds(first, 64 * MIX_PAIRS), :], spread, preferred_element_type=f32
        )
        matrices = jnp.where(keep, matrices, 0.0)
        for i in range(MIX_PAIRS):
            pair = t * MIX_PAIRS + i
            north = matrices[i * 64:i * 64 + 32]
            south = matrices[i * 64 + 32:i * 64 + 64]
            fold = jnp.concatenate([north + south, north - south], 0).astype(bf16)
            mine, theirs = own[pair], other[pair]
            values = jnp.concatenate([mine[0:32], theirs[0:32], mine[32:64], theirs[32:64]], 0)
            mixed = jnp.dot(fold, values, preferred_element_type=f32)
            stacked = jnp.concatenate(
                [mixed[0:32, :128], mixed[0:32, 128:], mixed[32:64, :128], mixed[32:64, 128:]], 0
            )
            turned = stacked.T
            rows_out[pl.ds(2 * pair, 64, stride=40), :] = turned[0:64]
            rows_out[pl.ds(2 * pair + 1, 64, stride=40), :] = turned[64:128]
        return carry

    lax.fori_loop(0, pairs // MIX_PAIRS, group_step, 0)
    out[...] = rows_out[...].astype(bf16)
    bring.wait()


def mix(inverses, own, other, table):
    return pl.pallas_call(
        mix_kernel,
        out_shape=[
            jax.ShapeDtypeStruct((2560, 128), bf16),
            jax.ShapeDtypeStruct(table.shape, table.dtype),
        ],
        in_specs=[pl.BlockSpec(memory_space=pltpu.VMEM)] * 3
        + [pl.BlockSpec(memory_space=pl.ANY)],
        out_specs=[pl.BlockSpec(memory_space=pltpu.VMEM)] * 2,
        scratch_shapes=[pltpu.VMEM((2560, 128), f32), pltpu.SemaphoreType.DMA],
        compiler_params=pltpu.CompilerParams(vmem_limit_bytes=MIX_VMEM),
        name="mix",
    )(inverses, own, other, table)


def legendre_kernel(waves, own, other, table, out, even, odd):
    slots, parities, degree_rows, pairs = table.shape
    slab = lax.axis_index("lev")
    owner = lax.axis_index("lat")
    row = iota((256, 256), 0)
    target = (
        ((row >> 6) & 1) * 128 + ((row >> 5) & 1) * 64 + ((row >> 7) ^ slab) * 32 + (row & 31)
    )
    order = (iota((256, 256), 1) == target).astype(f32).astype(bf16)
    both = jnp.concatenate([own[...], other[...]], 1)
    ordered = jnp.dot(both, order, preferred_element_type=f32)
    even[...] = ordered[:, :128]
    odd[...] = ordered[:, 128:]
    for s in range(slots):
        for q in range(parities):
            half = even if q == 0 else odd
            folded = half[pl.ds(s, pairs, stride=slots), :].astype(bf16)
            summed = jnp.dot(table[s, q], folded, preferred_element_type=f32)
            wave = waves[owner * slots + s]
            degree = wave + 2 * (slab * degree_rows + iota(summed.shape, 0)) + q
            out[s, q] = jnp.where(degree <= TRUNC, summed, 0.0).astype(bf16)


def legendre_sum(wave_table, own, other, table):
    slots, parities, degree_rows, pairs = table.shape
    return pl.pallas_call(
        legendre_kernel,
        out_shape=jax.ShapeDtypeStruct((slots, parities, degree_rows, 128), bf16),
        in_specs=[pl.BlockSpec(memory_space=pltpu.SMEM)]
        + [pl.BlockSpec(memory_space=pltpu.VMEM)] * 3,
        out_specs=pl.BlockSpec(memory_space=pltpu.VMEM),
        scratch_shapes=[pltpu.VMEM((slots * pairs, 128), f32)] * 2,
        compiler_params=pltpu.CompilerParams(vmem_limit_bytes=LEGENDRE_VMEM),
        name="legendre",
    )(wave_table, own, other, table)


def on_device(grid_values, lat_counts, wave_table, inverses, legendre):
    pair_total = lat_counts.shape[0]
    slab_width = grid_values.shape[1]
    grouped = grid_values.reshape(pair_total, 2 * slab_width, grid_values.shape[2])
    swap = [(0, 1), (1, 0)]
    own = fourier(grouped, lat_counts, wave_table)
    other = lax.ppermute(own, "lev", swap)
    half = lax.dynamic_slice_in_dim(inverses, lax.axis_index("lev") * 16, 16, 2)
    half = half.astype(bf16).transpose(0, 2, 1, 3).reshape(2 * pair_total * 32, 32)
    send, table = mix(half, own, other, legendre)
    slab = lax.all_to_all(
        send.reshape(64, 40, 128), "lat", split_axis=0, concat_axis=0, tiled=True
    )
    rest = lax.ppermute(slab, "lev", swap)
    return legendre_sum(wave_table, slab.reshape(2560, 128), rest.reshape(2560, 128), table)


def solution(mesh):
    placed = (
        P("lat", "lev", None),
        P("lat"),
        P(),
        P("lat", None, None, None),
        P("lat", None, "lev", None),
    )
    return jax.shard_map(
        on_device,
        mesh=mesh,
        in_specs=placed,
        out_specs=P("lat", None, "lev", None),
        check_vma=False,
    )
```

time: 992 us -> 45.6 us (0.05)
  other arithmetic: 764 us -> 0.77 us
  local copies, waits for them, and re-layouts: 88.3 us -> 0.55 us
  matrix products: 38.9 us -> 0 us
  loops' own time: 38 us -> 0 us
  waiting for transfers between devices: 21.7 us -> 2.89 us
  between operations: 13.5 us -> 0.04 us
  Pallas kernels: 0 us -> 13 us
    another operation x20 -> x0, other arithmetic: 751 us -> none
    dot_general x22 -> x0, matrix products: 38.9 us -> none  [the longest x20 34 us: transform(): product = jnp.dot(pair_rows, basis, preferred_element_type=jnp.float32)]
    another operation x1 -> x0, loops' own time: 38 us -> none  [on_device(): lax.map(transform, (grouped, lat_counts))]
    dynamic_slice x21 -> x0, local copies, waits for them, and re-layouts: 26.2 us -> none  [the longest x20 26.2 us: on_device(): lax.map(transform, (grouped, lat_counts))]
    all_gather x2 -> x0, waiting for transfers between devices: 21.6 us -> none  [the longest x1 12.4 us: on_device(): every_level = lax.all_gather(fourier, 'lev', axis=1, tiled=True)]
    unnamed x7 -> x4, local copies, waits for them, and re-layouts: 14.8 us -> 0.01 us
    reshape x2 -> x0, local copies, waits for them, and re-layouts: 13.9 us -> none  [fold_pairs(): paired = owned.reshape(wave_count, all_lats // 2, 2, 2 * columns)]
    dynamic_update_slice x20 -> x0, local copies, waits for them, and re-layouts: 13.3 us -> none  [on_device(): lax.map(transform, (grouped, lat_counts))]
  transfers between devices with their start and end apart: 2 -> 2, of which waited for: 2 -> 2; matrix products, arithmetic and copies ran while one was open for 0% -> 1% of each run, Pallas kernels for 0% -> 0%
where the time goes in v2:
time: 45.6 us; the launch traced here: 45.5 us
  blocking collectives  24.9 us (55%)
  Pallas kernels  13 us (29%)
  starting transfers between devices  3.34 us (7%)
  waiting for transfers between devices  2.89 us (6%)
  other arithmetic  0.77 us (2%)
  local copies, waits for them, and re-layouts  0.55 us (1%)
    all_to_all x1, blocking collectives, on_device(): lax.all_to_all(send.reshape(64, 40, 128), 'lat', split_axis=0, concat_axi...  24.9 us
    pallas_call x1, Pallas kernels, fourier(): pl.pallas_call(fourier_kernel, out_shape=jax.ShapeDtypeStruct((pairs, row...  7.62 us
    pallas_call x1, Pallas kernels, legendre_sum(): pl.pallas_call(legendre_kernel, out_shape=jax.ShapeDtypeStruct((slots, pa...  3.44 us
    pallas_call x1, Pallas kernels, mix(): pl.pallas_call(mix_kernel, out_shape=[jax.ShapeDtypeStruct((2560, 128), b...  1.93 us
    ppermute x1, starting transfers between devices, on_device(): rest = lax.ppermute(slab, 'lev', swap)  1.84 us
    ppermute x1, waiting for transfers between devices, on_device(): rest = lax.ppermute(slab, 'lev', swap)  1.72 us
    ppermute x1, starting transfers between devices, on_device(): other = lax.ppermute(own, 'lev', swap)  1.5 us
    ppermute x1, waiting for transfers between devices, on_device(): other = lax.ppermute(own, 'lev', swap)  1.16 us
  transfers between devices with their start and end apart: 2, of which 2 were waited for; matrix products, arithmetic and copies ran while one was open for 1% of the time, Pallas kernels for 0%

profile of v2, /device:TPU:1, one launch (start us, length us, event | category | flops | bytes accessed | tf_op | source)
XLA Modules:
  0.0 45.5 jit_solution(14482307463207041766)
XLA Ops:
  0.0 0.0 copy-start
  0.0 0.8 %pad_add_fusion = s32[148]{0:T(256)S(1)} fusion(s32[20]{0:T(128)} %param.6, s32[128]{0:T(128)} %waves.1), kind=kLoop, calls=%fused_computation.2 | loop fusion | flops 148 | bytes 1184 | tf_op jit(solution)/shard_map/concatenate | solution.py:136
  0.8 7.6 %fourier.1.own = bf16[20,64,256]{2,1,0:T(8,128)(2,1)S(1)} custom-call(s32[256]{0:T(256)S(1)} %pad.4.numbers, s32[1,256]{1,0:T(1,128)S(1)} %bitcast.12, bf16[20,64,5136]{2,1,0:T(8,128)(2,1)} %bitcast.13), custom_call_target="tpu_custom_call" | custom-call | tf_op jit(solution)/shard_map/fourier/pallas_call | solution.py:137
  8.4 1.5 %collective-permute-start = (bf16[20,64,256]{2,1,0:T(8,128)(2,1)S(1)}, bf16[20,64,256]{2,1,0:T(8,128)(2,1)S(1)}, u32[]{:S(2)}, u32[]{:S(2)}) collective-permute-start(bf16[20,64,256]{2,1,0:T(8,128)(2,1)S(1)} %fourier.1.own), channel_id=1, source_target_pairs={{0,1},{1,0},{2,3},{3,2},{4,5},{5,4},{6,7},{7,6},{8,9},{9,8},{10,11... | collective-permute-start | bytes 1966088 | tf_op jit(solution)/shard_map/ppermute | solution.py:256
  9.9 0.0 copy-done
  9.9 0.0 copy-start.1
  10.0 0.5 %copy.6 = bf16[40,16,2,32]{3,2,1,0:T(2,128)(2,1)S(1)} copy(bf16[40,16,2,32]{0,3,1,2:T(8,128)(2,1)S(1)} %fusion) | data formatting | bytes 163840 | tf_op jit(solution)/shard_map/transpose | solution.py:258
  10.5 1.2 %collective-permute-done.other = bf16[20,64,256]{2,1,0:T(8,128)(2,1)S(1)} collective-permute-done((bf16[20,64,256]{2,1,0:T(8,128)(2,1)S(1)}, bf16[20,64,256]{2,1,0:T(8,128)(2,1)S(1)}, u32[]{:S(2)}, u32[]{:S(2)}) %collective-permute-start) | collective-permute-done | bytes 655392 | tf_op jit(solution)/shard_map/ppermute | solution.py:256
  11.6 1.9 %mix.1 = (bf16[2560,128]{1,0:T(8,128)(2,1)S(1)}, bf16[2,2,320,1280]{3,2,1,0:T(8,128)(2,1)S(1)}) custom-call(bf16[1280,32]{1,0:T(8,128)(2,1)S(1)} %bitcast.9, bf16[20,64,256]{2,1,0:T(8,128)(2,1)S(1)} %fourier.1.own, bf16[20,64,256]{2,1,0:T(8,128)(2,1)S(1)} %collective-permute-done.other, bf16[2,2,320,1280]{3,2,1,0:T(8,128)(2,1)} %table.1), custom_call_target="tpu_custom_call" | custom-call | tf_op jit(solution)/shard_map/mix/pallas_call | solution.py:198
  13.6 24.9 %all_to_all.5 = bf16[64,40,128]{2,1,0:T(8,128)(2,1)S(1)} all-to-all(bf16[64,40,128]{2,1,0:T(8,128)(2,1)S(1)} %bitcast.11), channel_id=1, replica_groups=mesh['lat'=64,'lev'=2] {'lat'}, dimensions={0} | all-to-all | bytes 1310720 | tf_op jit(solution)/shard_map/all_to_all | solution.py:260
  38.5 1.8 %collective-permute-start.1 = (bf16[64,40,128]{2,1,0:T(8,128)(2,1)S(1)}, bf16[64,40,128]{2,1,0:T(8,128)(2,1)S(1)}, u32[]{:S(2)}, u32[]{:S(2)}) collective-permute-start(bf16[64,40,128]{2,1,0:T(8,128)(2,1)S(1)} %all_to_all.5), channel_id=1, source_target_pairs={{0,1},{1,0},{2,3},{3,2},{4,5},{5,4},{6,7},{7,6},{8,9},{9,8},{10,11... | collective-permute-start | bytes 1966088 | tf_op jit(solution)/shard_map/ppermute | solution.py:263
  40.3 1.7 %collective-permute-done.1 = bf16[64,40,128]{2,1,0:T(8,128)(2,1)S(1)} collective-permute-done((bf16[64,40,128]{2,1,0:T(8,128)(2,1)S(1)}, bf16[64,40,128]{2,1,0:T(8,128)(2,1)S(1)}, u32[]{:S(2)}, u32[]{:S(2)}) %collective-permute-start.1) | collective-permute-done | bytes 655392 | tf_op jit(solution)/shard_map/ppermute | solution.py:263
  42.0 0.0 copy-done.1
  42.0 3.4 %legendre.1 = bf16[2,2,320,128]{3,2,1,0:T(8,128)(2,1)} custom-call(s32[128]{0:T(128)S(1)} %copy-done.1, bf16[2560,128]{1,0:T(8,128)(2,1)S(1)} %bitcast.8, bf16[2560,128]{1,0:T(8,128)(2,1)S(1)} %bitcast.10, bf16[2,2,320,1280]{3,2,1,0:T(8,128)(2,1)S(1)} %get-tuple-element.8.table), custom_call_target="tpu_custom_call" | custom-call | tf_op jit(solution)/shard_map/legendre/pallas_call | solution.py:238
  (2 shorter events, 0.0 us)
Async XLA Ops:
  0.0 9.9 %copy-start = (f32[40,2,32,32]{0,3,2,1:T(8,128)S(1)}, f32[40,2,32,32]{0,3,2,1:T(8,128)}, u32[]{:S(2)}) copy-start(f32[40,2,32,32]{0,3,2,1:T(8,128)} %param.8) | copy-start | bytes 983044
  8.4 3.2 %collective-permute-start = (bf16[20,64,256]{2,1,0:T(8,128)(2,1)S(1)}, bf16[20,64,256]{2,1,0:T(8,128)(2,1)S(1)}, u32[]{:S(2)}, u32[]{:S(2)}) collective-permute-start(bf16[20,64,256]{2,1,0:T(8,128)(2,1)S(1)} %fourier.1.own), channel_id=1, source_target_pairs={{0,1},{1,0},{2,3},{3,2},{4,5},{5,4},{6,7},{7,6},{8,9},{9,8},{10,11... | collective-permute-start | bytes 1966088 | tf_op jit(solution)/shard_map/ppermute | solution.py:256
  9.9 32.1 %copy-start.1 = (s32[128]{0:T(128)S(1)}, s32[128]{0:T(128)}, u32[]{:S(2)}) copy-start(s32[128]{0:T(128)} %waves.1) | copy-start | bytes 1540
  38.5 3.6 %collective-permute-start.1 = (bf16[64,40,128]{2,1,0:T(8,128)(2,1)S(1)}, bf16[64,40,128]{2,1,0:T(8,128)(2,1)S(1)}, u32[]{:S(2)}, u32[]{:S(2)}) collective-permute-start(bf16[64,40,128]{2,1,0:T(8,128)(2,1)S(1)} %all_to_all.5), channel_id=1, source_target_pairs={{0,1},{1,0},{2,3},{3,2},{4,5},{5,4},{6,7},{7,6},{8,9},{9,8},{10,11... | collective-permute-start | bytes 1966088 | tf_op jit(solution)/shard_map/ppermute | solution.py:263

commit v3 on v2

--- a/solution.py
+++ b/solution.py
@@ -11,9 +11,9 @@
 BLOCK = 256
 GROUP = 4
 AHEAD = 8
-MIX_PAIRS = 5
 FOURIER_VMEM = 53 * 2**20
-MIX_VMEM = 48 * 2**20
+FOLD_VMEM = 50 * 2**20
+PREPARE_VMEM = 48 * 2**20
 LEGENDRE_VMEM = 24 * 2**20
 
 COS_TERMS = (1.0, -19.73920440673828, 64.9391098022461, -85.45005798339844,
@@ -155,96 +155,137 @@
     )(numbers, numbers.reshape(1, 256), grouped)
 
 
-def mix_kernel(inverses, own, other, table, out, table_out, rows_out, sem):
-    bring = pltpu.make_async_copy(table, table_out, sem)
+def fold_kernel(inverses, table, out, table_out, sem):
+    bring = pltpu.make_async_copy(table.at[0], table_out, sem)
     bring.start()
     slab = lax.axis_index("lev")
-    pairs = own.shape[0]
     lane = iota((32, 128), 1)
     level = (((lane >> 5) & 1) ^ slab) * 16 + ((lane >> 1) & 15)
     spread = (iota((32, 128), 0) == level).astype(f32).astype(bf16)
-    row = iota((64 * MIX_PAIRS, 128), 0)
-    lane = iota((64 * MIX_PAIRS, 128), 1)
+    matrices = jnp.dot(inverses[...], spread, preferred_element_type=f32)
+    row = iota(matrices.shape, 0)
+    lane = iota(matrices.shape, 1)
     keep = ((row & 1) == (lane & 1)) & (((row >> 5) & 1) == (lane >> 6))
-
-    def group_step(t, carry):
-        first = pl.multiple_of(t * 64 * MIX_PAIRS, 64 * MIX_PAIRS)
-        matrices = jnp.dot(
-            inverses[pl.ds(first, 64 * MIX_PAIRS), :], spread, preferred_element_type=f32
+    matrices = jnp.where(keep, matrices, 0.0)
+    for pair in range(out.shape[0]):
+        north = matrices[pair * 64:pair * 64 + 32]
+        south = matrices[pair * 64 + 32:pair * 64 + 64]
+        out[pair] = jnp.concatenate([north + south, north - south], 0).astype(bf16)
+    bring.wait()
+
+
+def fold_matrices(inverses, table):
+    return pl.pallas_call(
+        fold_kernel,
+        out_shape=[
+            jax.ShapeDtypeStruct((inverses.shape[0] // 64, 64, 128), bf16),
+            jax.ShapeDtypeStruct(table.shape[1:], table.dtype),
+        ],
+        in_specs=[pl.BlockSpec(memory_space=pltpu.VMEM), pl.BlockSpec(memory_space=pl.ANY)],
+        out_specs=[pl.BlockSpec(memory_space=pltpu.VMEM)] * 2,
+        scratch_shapes=[pltpu.SemaphoreType.DMA],
+        compiler_params=pltpu.CompilerParams(vmem_limit_bytes=FOLD_VMEM),
+        cost_estimate=pl.CostEstimate(flops=2**24, bytes_accessed=2**22, transcendentals=0),
+        name="fold",
+    )(inverses, table)
+
+
+def mix_kernel(matrices, own, other, out, rows_out):
+    for pair in range(own.shape[0]):
+        mine, theirs = own[pair], other[pair]
+        values = jnp.concatenate([mine[0:32], theirs[0:32], mine[32:64], theirs[32:64]], 0)
+        mixed = jnp.dot(matrices[pair], values, preferred_element_type=f32)
+        stacked = jnp.concatenate(
+            [mixed[0:32, :128], mixed[0:32, 128:], mixed[32:64, :128], mixed[32:64, 128:]], 0
         )
-        matrices = jnp.where(keep, matrices, 0.0)
-        for i in range(MIX_PAIRS):
-            pair = t * MIX_PAIRS + i
-            north = matrices[i * 64:i * 64 + 32]
-            south = matrices[i * 64 + 32:i * 64 + 64]
-            fold = jnp.concatenate([north + south, north - south], 0).astype(bf16)
-            mine, theirs = own[pair], other[pair]
-            values = jnp.concatenate([mine[0:32], theirs[0:32], mine[32:64], theirs[32:64]], 0)
-            mixed = jnp.dot(fold, values, preferred_element_type=f32)
-            stacked = jnp.concatenate(
-                [mixed[0:32, :128], mixed[0:32, 128:], mixed[32:64, :128], mixed[32:64, 128:]], 0
-            )
-            turned = stacked.T
-            rows_out[pl.ds(2 * pair, 64, stride=40), :] = turned[0:64]
-            rows_out[pl.ds(2 * pair + 1, 64, stride=40), :] = turned[64:128]
-        return carry
-
-    lax.fori_loop(0, pairs // MIX_PAIRS, group_step, 0)
+        turned = stacked.T
+        rows_out[pl.ds(2 * pair, 64, stride=40), :] = turned[0:64]
+        rows_out[pl.ds(2 * pair + 1, 64, stride=40), :] = turned[64:128]
     out[...] = rows_out[...].astype(bf16)
+
+
+def mix(matrices, own, other):
+    return pl.pallas_call(
+        mix_kernel,
+        out_shape=jax.ShapeDtypeStruct((2560, 128), bf16),
+        in_specs=[pl.BlockSpec(memory_space=pltpu.VMEM)] * 3,
+        out_specs=pl.BlockSpec(memory_space=pltpu.VMEM),
+        scratch_shapes=[pltpu.VMEM((2560, 128), f32)],
+        compiler_params=pltpu.CompilerParams(vmem_limit_bytes=LEGENDRE_VMEM),
+        name="mix",
+    )(matrices, own, other)
+
+
+def unfold(values, side, even, odd):
+    slab = lax.axis_index("lev") ^ side
+    row = iota((128, 256), 0)
+    target = (row >> 6) * 128 + ((row >> 5) & 1) * 64 + slab * 32 + (row & 31)
+    order = (iota((128, 256), 1) == target).astype(f32).astype(bf16)
+    ordered = jnp.dot(values, order, preferred_element_type=f32)
+    even[...] = ordered[:, :128]
+    odd[...] = ordered[:, 128:]
+
+
+def prepare_kernel(own, table, out, table_out, even, odd, sem):
+    bring = pltpu.make_async_copy(table.at[1], table_out, sem)
+    bring.start()
+    slots, parities, pairs, _ = out.shape
+    unfold(own[...], 0, even, odd)
+    for s in range(slots):
+        out[s, 0] = even[pl.ds(s, pairs, stride=slots), :].astype(bf16)
+        out[s, 1] = odd[pl.ds(s, pairs, stride=slots), :].astype(bf16)
     bring.wait()
 
 
-def mix(inverses, own, other, table):
-    return pl.pallas_call(
-        mix_kernel,
+def prepare(own, table):
+    slots, parities, _, pairs = table.shape
+    return pl.pallas_call(
+        prepare_kernel,
         out_shape=[
-            jax.ShapeDtypeStruct((2560, 128), bf16),
-            jax.ShapeDtypeStruct(table.shape, table.dtype),
+            jax.ShapeDtypeStruct((slots, parities, pairs, 128), bf16),
+            jax.ShapeDtypeStruct(table.shape[1:], table.dtype),
         ],
-        in_specs=[pl.BlockSpec(memory_space=pltpu.VMEM)] * 3
-        + [pl.BlockSpec(memory_space=pl.ANY)],
+        in_specs=[pl.BlockSpec(memory_space=pltpu.VMEM), pl.BlockSpec(memory_space=pl.ANY)],
         out_specs=[pl.BlockSpec(memory_space=pltpu.VMEM)] * 2,
-        scratch_shapes=[pltpu.VMEM((2560, 128), f32), pltpu.SemaphoreType.DMA],
-        compiler_params=pltpu.CompilerParams(vmem_limit_bytes=MIX_VMEM),
-        name="mix",
-    )(inverses, own, other, table)
-
-
-def legendre_kernel(waves, own, other, table, out, even, odd):
-    slots, parities, degree_rows, pairs = table.shape
+        scratch_shapes=[pltpu.VMEM((slots * pairs, 128), f32)] * 2 + [pltpu.SemaphoreType.DMA],
+        compiler_params=pltpu.CompilerParams(vmem_limit_bytes=PREPARE_VMEM),
+        cost_estimate=pl.CostEstimate(
+            flops=4 * slots * pairs * 128 * 128, bytes_accessed=2**22, transcendentals=0
+        ),
+        name="prepare",
+    )(own, table)
+
+
+def legendre_kernel(waves, folded, other, first_table, second_table, out, even, odd):
+    slots, parities, degree_rows, _ = out.shape
+    pairs = folded.shape[2]
     slab = lax.axis_index("lev")
     owner = lax.axis_index("lat")
-    row = iota((256, 256), 0)
-    target = (
-        ((row >> 6) & 1) * 128 + ((row >> 5) & 1) * 64 + ((row >> 7) ^ slab) * 32 + (row & 31)
-    )
-    order = (iota((256, 256), 1) == target).astype(f32).astype(bf16)
-    both = jnp.concatenate([own[...], other[...]], 1)
-    ordered = jnp.dot(both, order, preferred_element_type=f32)
-    even[...] = ordered[:, :128]
-    odd[...] = ordered[:, 128:]
+    unfold(other[...], 1, even, odd)
     for s in range(slots):
+        mine = iota((1, 128), 1) == owner * slots + s
+        wave = jnp.sum(jnp.where(mine, waves[...], 0), axis=1, keepdims=True)
+        table = (first_table, second_table)[s]
         for q in range(parities):
             half = even if q == 0 else odd
-            folded = half[pl.ds(s, pairs, stride=slots), :].astype(bf16)
-            summed = jnp.dot(table[s, q], folded, preferred_element_type=f32)
-            wave = waves[owner * slots + s]
+            both = folded[s, q] + half[pl.ds(s, pairs, stride=slots), :].astype(bf16)
+            summed = jnp.dot(table[q], both, preferred_element_type=f32)
             degree = wave + 2 * (slab * degree_rows + iota(summed.shape, 0)) + q
             out[s, q] = jnp.where(degree <= TRUNC, summed, 0.0).astype(bf16)
 
 
-def legendre_sum(wave_table, own, other, table):
-    slots, parities, degree_rows, pairs = table.shape
+def legendre_sum(wave_table, folded, other, first_table, second_table):
+    slots, parities, pairs, _ = folded.shape
+    degree_rows = first_table.shape[1]
     return pl.pallas_call(
         legendre_kernel,
         out_shape=jax.ShapeDtypeStruct((slots, parities, degree_rows, 128), bf16),
-        in_specs=[pl.BlockSpec(memory_space=pltpu.SMEM)]
-        + [pl.BlockSpec(memory_space=pltpu.VMEM)] * 3,
+        in_specs=[pl.BlockSpec(memory_space=pltpu.VMEM)] * 5,
         out_specs=pl.BlockSpec(memory_space=pltpu.VMEM),
         scratch_shapes=[pltpu.VMEM((slots * pairs, 128), f32)] * 2,
         compiler_params=pltpu.CompilerParams(vmem_limit_bytes=LEGENDRE_VMEM),
         name="legendre",
-    )(wave_table, own, other, table)
+    )(wave_table.reshape(1, 128), folded, other, first_table, second_table)
 
 
 def on_device(grid_values, lat_counts, wave_table, inverses, legendre):
@@ -256,12 +297,16 @@
     other = lax.ppermute(own, "lev", swap)
     half = lax.dynamic_slice_in_dim(inverses, lax.axis_index("lev") * 16, 16, 2)
     half = half.astype(bf16).transpose(0, 2, 1, 3).reshape(2 * pair_total * 32, 32)
-    send, table = mix(half, own, other, legendre)
+    matrices, first_table = fold_matrices(half, legendre)
+    send = mix(matrices, own, other)
     slab = lax.all_to_all(
         send.reshape(64, 40, 128), "lat", split_axis=0, concat_axis=0, tiled=True
     )
     rest = lax.ppermute(slab, "lev", swap)
-    return legendre_sum(wave_table, slab.reshape(2560, 128), rest.reshape(2560, 128), table)
+    folded, second_table = prepare(slab.reshape(2560, 128), legendre)
+    return legendre_sum(
+        wave_table, folded, rest.reshape(2560, 128), first_table, second_table
+    )
 
 
 def solution(mesh):

time: 45.6 us -> 44 us (0.965)
  waiting for transfers between devices: 2.89 us -> 0.26 us
  Pallas kernels: 13 us -> 14 us
    pallas_call x1 -> x3, Pallas kernels: 1.93 us -> 3.51 us  [the longest x1 1.45 us: prepare(): pl.pallas_call(prepare_kernel, out_shape=[jax.ShapeDtypeStruct((slots, pa...]
    ppermute x1, waiting for transfers between devices: 1.72 us -> 0.26 us  [on_device(): rest = lax.ppermute(slab, 'lev', swap)]
    ppermute x1, waiting for transfers between devices: 1.16 us -> 0.01 us  [on_device(): other = lax.ppermute(own, 'lev', swap)]
    pallas_call x1, Pallas kernels: 3.44 us -> 2.85 us  [legendre_sum(): pl.pallas_call(legendre_kernel, out_shape=jax.ShapeDtypeStruct((slots, pa...]
  transfers between devices with their start and end apart: 2 -> 2, of which waited for: 2 -> 1; matrix products, arithmetic and copies ran while one was open for 1% -> 1% of each run, Pallas kernels for 0% -> 7%
where the time goes in v3:
time: 44 us; the launch traced here: 43.8 us
  blocking collectives  25.1 us (57%)
  Pallas kernels  14 us (32%)
  starting transfers between devices  3.09 us (7%)
  other arithmetic  0.77 us (2%)
  local copies, waits for them, and re-layouts  0.55 us (1%)
    all_to_all x1, blocking collectives, on_device(): lax.all_to_all(send.reshape(64, 40, 128), 'lat', split_axis=0, concat_axi...  25.1 us
    pallas_call x1, Pallas kernels, fourier(): pl.pallas_call(fourier_kernel, out_shape=jax.ShapeDtypeStruct((pairs, row...  7.62 us
    pallas_call x1, Pallas kernels, legendre_sum(): pl.pallas_call(legendre_kernel, out_shape=jax.ShapeDtypeStruct((slots, pa...  2.85 us
    ppermute x1, starting transfers between devices, on_device(): rest = lax.ppermute(slab, 'lev', swap)  1.59 us
    ppermute x1, starting transfers between devices, on_device(): other = lax.ppermute(own, 'lev', swap)  1.5 us
    pallas_call x1, Pallas kernels, prepare(): pl.pallas_call(prepare_kernel, out_shape=[jax.ShapeDtypeStruct((slots, pa...  1.45 us
    pallas_call x1, Pallas kernels, fold_matrices(): pl.pallas_call(fold_kernel, out_shape=[jax.ShapeDtypeStruct((inverses.sha...  1.44 us
  transfers between devices with their start and end apart: 2, of which 1 were waited for; matrix products, arithmetic and copies ran while one was open for 1% of the time, Pallas kernels for 7%

profile of v3, /device:TPU:1, one launch (start us, length us, event | category | flops | bytes accessed | tf_op | source)
XLA Modules:
  0.0 43.8 jit_solution(5897494261396601030)
XLA Ops:
  0.0 0.0 copy-start
  0.0 0.8 %pad_add_fusion = s32[148]{0:T(256)S(1)} fusion(s32[20]{0:T(128)} %param.6, s32[128]{0:T(128)} %param.7), kind=kLoop, calls=%fused_computation.2 | loop fusion | flops 148 | bytes 1184 | tf_op jit(solution)/shard_map/concatenate | solution.py:136
  0.8 7.6 %fourier.1.own = bf16[20,64,256]{2,1,0:T(8,128)(2,1)S(1)} custom-call(s32[256]{0:T(256)S(1)} %pad.4.numbers, s32[1,256]{1,0:T(1,128)S(1)} %bitcast.13, bf16[20,64,5136]{2,1,0:T(8,128)(2,1)} %bitcast.15), custom_call_target="tpu_custom_call" | custom-call | tf_op jit(solution)/shard_map/fourier/pallas_call | solution.py:137
  8.4 1.5 %collective-permute-start = (bf16[20,64,256]{2,1,0:T(8,128)(2,1)S(1)}, bf16[20,64,256]{2,1,0:T(8,128)(2,1)S(1)}, u32[]{:S(2)}, u32[]{:S(2)}) collective-permute-start(bf16[20,64,256]{2,1,0:T(8,128)(2,1)S(1)} %fourier.1.own), channel_id=1, source_target_pairs={{0,1},{1,0},{2,3},{3,2},{4,5},{5,4},{6,7},{7,6},{8,9},{9,8},{10,11... | collective-permute-start | bytes 1966088 | tf_op jit(solution)/shard_map/ppermute | solution.py:297
  9.9 0.0 copy-done
  9.9 0.5 %copy.6 = bf16[40,16,2,32]{3,2,1,0:T(2,128)(2,1)S(1)} copy(bf16[40,16,2,32]{0,3,1,2:T(8,128)(2,1)S(1)} %fusion) | data formatting | bytes 163840 | tf_op jit(solution)/shard_map/transpose | solution.py:299
  10.4 1.4 %fold.1 = (bf16[20,64,128]{2,1,0:T(8,128)(2,1)S(1)}, bf16[2,320,1280]{2,1,0:T(8,128)(2,1)S(1)}) custom-call(bf16[1280,32]{1,0:T(8,128)(2,1)S(1)} %bitcast.11, bf16[2,2,320,1280]{3,2,1,0:T(8,128)(2,1)} %table.3), custom_call_target="tpu_custom_call" | custom-call | flops 16777216 | bytes 4194304 | tf_op jit(solution)/shard_map/fold/pallas_call | solution.py:178
  11.9 0.0 collective-permute-done.other
  11.9 0.6 %mix.1 = bf16[2560,128]{1,0:T(8,128)(2,1)S(1)} custom-call(bf16[20,64,128]{2,1,0:T(8,128)(2,1)S(1)} %get-tuple-element.9.matrices, bf16[20,64,256]{2,1,0:T(8,128)(2,1)S(1)} %fourier.1.own, bf16[20,64,256]{2,1,0:T(8,128)(2,1)S(1)} %collective-permute-done.other), custom_call_target="tpu_custom_call" | custom-call | tf_op jit(solution)/shard_map/mix/pallas_call | solution.py:208
  12.5 25.1 %all_to_all.5 = bf16[64,40,128]{2,1,0:T(8,128)(2,1)S(1)} all-to-all(bf16[64,40,128]{2,1,0:T(8,128)(2,1)S(1)} %bitcast.9), channel_id=1, replica_groups=mesh['lat'=64,'lev'=2] {'lat'}, dimensions={0} | all-to-all | bytes 1310720 | tf_op jit(solution)/shard_map/all_to_all | solution.py:302
  37.7 1.6 %collective-permute-start.1 = (bf16[64,40,128]{2,1,0:T(8,128)(2,1)S(1)}, bf16[64,40,128]{2,1,0:T(8,128)(2,1)S(1)}, u32[]{:S(2)}, u32[]{:S(2)}) collective-permute-start(bf16[64,40,128]{2,1,0:T(8,128)(2,1)S(1)} %all_to_all.5), channel_id=1, source_target_pairs={{0,1},{1,0},{2,3},{3,2},{4,5},{5,4},{6,7},{7,6},{8,9},{9,8},{10,11... | collective-permute-start | bytes 1966088 | tf_op jit(solution)/shard_map/ppermute | solution.py:305
  39.3 0.0 copy-start.1
  39.3 1.5 %prepare.1 = (bf16[2,2,1280,128]{3,2,1,0:T(8,128)(2,1)S(1)}, bf16[2,320,1280]{2,1,0:T(8,128)(2,1)S(1)}) custom-call(bf16[2560,128]{1,0:T(8,128)(2,1)S(1)} %bitcast.10, bf16[2,2,320,1280]{3,2,1,0:T(8,128)(2,1)} %table.3), custom_call_target="tpu_custom_call" | custom-call | flops 167772160 | bytes 4194304 | tf_op jit(solution)/shard_map/prepare/pallas_call | solution.py:242
  40.7 0.3 collective-permute-done.1
  41.0 0.0 copy-done.1
  41.0 2.8 %legendre.1 = bf16[2,2,320,128]{3,2,1,0:T(8,128)(2,1)} custom-call(s32[1,128]{1,0:T(1,128)S(1)} %bitcast.14, bf16[2,2,1280,128]{3,2,1,0:T(8,128)(2,1)S(1)} %get-tuple-element.10.folded, bf16[2560,128]{1,0:T(8,128)(2,1)S(1)} %bitcast.12, bf16[2,320,1280]{2,1,0:T(8,128)(2,1)S(1)} %get-tuple-element.11.first_table, ...), custom_call_target="tpu_custom_call" | custom-call | tf_op jit(solution)/shard_map/legendre/pallas_call | solution.py:280
  (2 shorter events, 0.0 us)
Async XLA Ops:
  0.0 9.9 %copy-start = (f32[40,2,32,32]{0,3,2,1:T(8,128)S(1)}, f32[40,2,32,32]{0,3,2,1:T(8,128)}, u32[]{:S(2)}) copy-start(f32[40,2,32,32]{0,3,2,1:T(8,128)} %param.8) | copy-start | bytes 983044
  8.4 3.5 %collective-permute-start = (bf16[20,64,256]{2,1,0:T(8,128)(2,1)S(1)}, bf16[20,64,256]{2,1,0:T(8,128)(2,1)S(1)}, u32[]{:S(2)}, u32[]{:S(2)}) collective-permute-start(bf16[20,64,256]{2,1,0:T(8,128)(2,1)S(1)} %fourier.1.own), channel_id=1, source_target_pairs={{0,1},{1,0},{2,3},{3,2},{4,5},{5,4},{6,7},{7,6},{8,9},{9,8},{10,11... | collective-permute-start | bytes 1966088 | tf_op jit(solution)/shard_map/ppermute | solution.py:297
  37.7 3.3 %collective-permute-start.1 = (bf16[64,40,128]{2,1,0:T(8,128)(2,1)S(1)}, bf16[64,40,128]{2,1,0:T(8,128)(2,1)S(1)}, u32[]{:S(2)}, u32[]{:S(2)}) collective-permute-start(bf16[64,40,128]{2,1,0:T(8,128)(2,1)S(1)} %all_to_all.5), channel_id=1, source_target_pairs={{0,1},{1,0},{2,3},{3,2},{4,5},{5,4},{6,7},{7,6},{8,9},{9,8},{10,11... | collective-permute-start | bytes 1966088 | tf_op jit(solution)/shard_map/ppermute | solution.py:305
  39.3 1.7 %copy-start.1 = (s32[128]{0:T(128)S(1)}, s32[128]{0:T(128)}, u32[]{:S(2)}) copy-start(s32[128]{0:T(128)} %param.7) | copy-start | bytes 1540

commit v4 on v3

--- a/solution.py
+++ b/solution.py
@@ -12,7 +12,7 @@
 GROUP = 4
 AHEAD = 8
 FOURIER_VMEM = 53 * 2**20
-FOLD_VMEM = 50 * 2**20
+FOLD_VMEM = 51 * 2**20
 PREPARE_VMEM = 48 * 2**20
 LEGENDRE_VMEM = 24 * 2**20
 
@@ -36,9 +36,9 @@
     return lax.broadcasted_iota(jnp.int32, shape, dim)
 
 
-def fourier_kernel(numbers, waves, grid, out, values, bases, turns, tail, sems):
+def fourier_kernel(numbers, waves, grid, out, values, bases, turns, tail, scalars, sems, scalar_sem):
     pairs, rows, storage = grid.shape
-    counts = numbers.at[pl.ds(128, pairs)]
+    counts = scalars.at[pl.ds(128, pairs)]
     blocks = storage // BLOCK
     rest = storage - blocks * BLOCK
 
@@ -47,6 +47,8 @@
 
     for p in range(AHEAD):
         fetch(p).start()
+    bring = pltpu.make_async_copy(numbers, scalars, scalar_sem)
+    bring.start()
 
     table = jnp.broadcast_to(waves[:, 0:128], (8, 128))
     order = iota((128, 128), 0) == (iota((128, 128), 1) % 64) * 2 + iota((128, 128), 1) // 64
@@ -59,6 +61,7 @@
     position = jnp.where(row < 16, row, jnp.where(row < 32, (row - 16) * 16, BLOCK)).astype(f32)
     angle_index = position * wave_row
     lane = iota((16, BLOCK), 1).astype(f32).astype(bf16)
+    bring.wait()
 
     def make_basis(p):
         count_f = jnp.full((8, 128), counts[p], jnp.int32).astype(f32)
@@ -138,7 +141,7 @@
         fourier_kernel,
         out_shape=jax.ShapeDtypeStruct((pairs, rows, 256), bf16),
         in_specs=[
-            pl.BlockSpec(memory_space=pltpu.SMEM),
+            pl.BlockSpec(memory_space=pl.ANY),
             pl.BlockSpec(memory_space=pltpu.VMEM),
             pl.BlockSpec(memory_space=pl.ANY),
         ],
@@ -148,7 +151,9 @@
             pltpu.VMEM((pairs, BLOCK, 256), bf16),
             pltpu.VMEM((pairs, 24, 128), f32),
             pltpu.VMEM((GROUP, rows, BLOCK), bf16),
+            pltpu.SMEM((256,), jnp.int32),
             pltpu.SemaphoreType.DMA((pairs,)),
+            pltpu.SemaphoreType.DMA,
         ],
         compiler_params=pltpu.CompilerParams(vmem_limit_bytes=FOURIER_VMEM),
         name="fourier",
@@ -156,7 +161,7 @@
 
 
 def fold_kernel(inverses, table, out, table_out, sem):
-    bring = pltpu.make_async_copy(table.at[0], table_out, sem)
+    bring = pltpu.make_async_copy(table.at[0, 0], table_out, sem)
     bring.start()
     slab = lax.axis_index("lev")
     lane = iota((32, 128), 1)
@@ -179,7 +184,7 @@
         fold_kernel,
         out_shape=[
             jax.ShapeDtypeStruct((inverses.shape[0] // 64, 64, 128), bf16),
-            jax.ShapeDtypeStruct(table.shape[1:], table.dtype),
+            jax.ShapeDtypeStruct(table.shape[2:], table.dtype),
         ],
         in_specs=[pl.BlockSpec(memory_space=pltpu.VMEM), pl.BlockSpec(memory_space=pl.ANY)],
         out_specs=[pl.BlockSpec(memory_space=pltpu.VMEM)] * 2,
@@ -196,7 +201,7 @@
         values = jnp.concatenate([mine[0:32], theirs[0:32], mine[32:64], theirs[32:64]], 0)
         mixed = jnp.dot(matrices[pair], values, preferred_element_type=f32)
         stacked = jnp.concatenate(
-            [mixed[0:32, :128], mixed[0:32, 128:], mixed[32:64, :128], mixed[32:64, 128:]], 0
+            [mixed[0:32, :128], mixed[32:64, :128], mixed[0:32, 128:], mixed[32:64, 128:]], 0
         )
         turned = stacked.T
         rows_out[pl.ds(2 * pair, 64, stride=40), :] = turned[0:64]
@@ -216,25 +221,26 @@
     )(matrices, own, other)
 
 
-def unfold(values, side, even, odd):
-    slab = lax.axis_index("lev") ^ side
-    row = iota((128, 256), 0)
-    target = (row >> 6) * 128 + ((row >> 5) & 1) * 64 + slab * 32 + (row & 31)
-    order = (iota((128, 256), 1) == target).astype(f32).astype(bf16)
-    ordered = jnp.dot(values, order, preferred_element_type=f32)
-    even[...] = ordered[:, :128]
-    odd[...] = ordered[:, 128:]
-
-
-def prepare_kernel(own, table, out, table_out, even, odd, sem):
-    bring = pltpu.make_async_copy(table.at[1], table_out, sem)
-    bring.start()
+def unfold(rows, slab):
+    return rows, pltpu.roll(rows, jnp.where(slab == 0, 96, 32), 1)
+
+
+def prepare_kernel(own, table, out, table_out, rows, sems):
+    bring = [
+        pltpu.make_async_copy(table.at[0, 1], table_out.at[0], sems.at[0]),
+        pltpu.make_async_copy(table.at[1], table_out.at[pl.ds(1, 2)], sems.at[1]),
+    ]
+    for copy in bring:
+        copy.start()
     slots, parities, pairs, _ = out.shape
-    unfold(own[...], 0, even, odd)
+    slab = lax.axis_index("lev")
+    rows[...] = own[...].astype(f32)
     for s in range(slots):
-        out[s, 0] = even[pl.ds(s, pairs, stride=slots), :].astype(bf16)
-        out[s, 1] = odd[pl.ds(s, pairs, stride=slots), :].astype(bf16)
-    bring.wait()
+        same, opposite = unfold(rows[pl.ds(s, pairs, stride=slots), :], slab)
+        out[s, slab] = same.astype(bf16)
+        out[s, 1 - slab] = opposite.astype(bf16)
+    for copy in bring:
+        copy.wait()
 
 
 def prepare(own, table):
@@ -243,11 +249,13 @@
         prepare_kernel,
         out_shape=[
             jax.ShapeDtypeStruct((slots, parities, pairs, 128), bf16),
-            jax.ShapeDtypeStruct(table.shape[1:], table.dtype),
+            jax.ShapeDtypeStruct((3,) + table.shape[2:], table.dtype),
         ],
         in_specs=[pl.BlockSpec(memory_space=pltpu.VMEM), pl.BlockSpec(memory_space=pl.ANY)],
         out_specs=[pl.BlockSpec(memory_space=pltpu.VMEM)] * 2,
-        scratch_shapes=[pltpu.VMEM((slots * pairs, 128), f32)] * 2 + [pltpu.SemaphoreType.DMA],
+        scratch_shapes=[pltpu.VMEM((slots * pairs, 128), f32)] + [
+            pltpu.SemaphoreType.DMA((2,))
+        ],
         compiler_params=pltpu.CompilerParams(vmem_limit_bytes=PREPARE_VMEM),
         cost_estimate=pl.CostEstimate(
             flops=4 * slots * pairs * 128 * 128, bytes_accessed=2**22, transcendentals=0
@@ -256,33 +264,40 @@
     )(own, table)
 
 
-def legendre_kernel(waves, folded, other, first_table, second_table, out, even, odd):
+def legendre_kernel(waves, folded, other, first_table, second_table, out, rows, both):
     slots, parities, degree_rows, _ = out.shape
     pairs = folded.shape[2]
     slab = lax.axis_index("lev")
     owner = lax.axis_index("lat")
-    unfold(other[...], 1, even, odd)
+    rows[...] = other[...].astype(f32)
+    mine = (((iota((16, 128), 1) >> 5) & 1) == slab).astype(f32).astype(bf16) > 0
+    mine = jnp.broadcast_to(mine[0:1], (pairs, 128))
     for s in range(slots):
-        mine = iota((1, 128), 1) == owner * slots + s
-        wave = jnp.sum(jnp.where(mine, waves[...], 0), axis=1, keepdims=True)
-        table = (first_table, second_table)[s]
+        same, opposite = unfold(rows[pl.ds(s, pairs, stride=slots), :], 1 - slab)
+        both[s, 1 - slab] = jnp.where(mine, folded[s, 1 - slab], same.astype(bf16))
+        both[s, slab] = jnp.where(mine, folded[s, slab], opposite.astype(bf16))
+    for s in range(slots):
+        here = iota((1, 128), 1) == owner * slots + s
+        wave = jnp.sum(jnp.where(here, waves[...], 0), axis=1, keepdims=True)
         for q in range(parities):
-            half = even if q == 0 else odd
-            both = folded[s, q] + half[pl.ds(s, pairs, stride=slots), :].astype(bf16)
-            summed = jnp.dot(table[q], both, preferred_element_type=f32)
+            table = first_table[...] if s + q == 0 else second_table[s * parities + q - 1]
+            summed = jnp.dot(table, both[s, q], preferred_element_type=f32)
             degree = wave + 2 * (slab * degree_rows + iota(summed.shape, 0)) + q
             out[s, q] = jnp.where(degree <= TRUNC, summed, 0.0).astype(bf16)
 
 
 def legendre_sum(wave_table, folded, other, first_table, second_table):
     slots, parities, pairs, _ = folded.shape
-    degree_rows = first_table.shape[1]
+    degree_rows = first_table.shape[0]
     return pl.pallas_call(
         legendre_kernel,
         out_shape=jax.ShapeDtypeStruct((slots, parities, degree_rows, 128), bf16),
         in_specs=[pl.BlockSpec(memory_space=pltpu.VMEM)] * 5,
         out_specs=pl.BlockSpec(memory_space=pltpu.VMEM),
-        scratch_shapes=[pltpu.VMEM((slots * pairs, 128), f32)] * 2,
+        scratch_shapes=[
+            pltpu.VMEM((slots * pairs, 128), f32),
+            pltpu.VMEM((slots, parities, pairs, 128), bf16),
+        ],
         compiler_params=pltpu.CompilerParams(vmem_limit_bytes=LEGENDRE_VMEM),
         name="legendre",
     )(wave_table.reshape(1, 128), folded, other, first_table, second_table)

time: 44 us -> 42.8 us (0.973)
  Pallas kernels: 14 us -> 13 us
    pallas_call x1, Pallas kernels: 2.85 us -> 2.1 us  [legendre_sum(): pl.pallas_call(legendre_kernel, out_shape=jax.ShapeDtypeStruct((slots, pa...]
  transfers between devices with their start and end apart: 2 -> 2, of which waited for: 1 -> 0; matrix products, arithmetic and copies ran while one was open for 1% -> 1% of each run, Pallas kernels for 7% -> 7%
where the time goes in v4:
time: 42.8 us; the launch traced here: 42.6 us
  blocking collectives  24.9 us (58%)
  Pallas kernels  13 us (30%)
  starting transfers between devices  3.33 us (8%)
  other arithmetic  0.77 us (2%)
  local copies, waits for them, and re-layouts  0.55 us (1%)
    all_to_all x1, blocking collectives, on_device(): lax.all_to_all(send.reshape(64, 40, 128), 'lat', split_axis=0, concat_axi...  24.9 us
    pallas_call x1, Pallas kernels, fourier(): pl.pallas_call(fourier_kernel, out_shape=jax.ShapeDtypeStruct((pairs, row...  7.37 us
    pallas_call x1, Pallas kernels, legendre_sum(): pl.pallas_call(legendre_kernel, out_shape=jax.ShapeDtypeStruct((slots, pa...  2.1 us
    ppermute x1, starting transfers between devices, on_device(): rest = lax.ppermute(slab, 'lev', swap)  1.82 us
    pallas_call x1, Pallas kernels, prepare(): pl.pallas_call(prepare_kernel, out_shape=[jax.ShapeDtypeStruct((slots, pa...  1.72 us
    ppermute x1, starting transfers between devices, on_device(): other = lax.ppermute(own, 'lev', swap)  1.5 us
    pallas_call x1, Pallas kernels, fold_matrices(): pl.pallas_call(fold_kernel, out_shape=[jax.ShapeDtypeStruct((inverses.sha...  1.16 us
  transfers between devices with their start and end apart: 2, of which 0 were waited for; matrix products, arithmetic and copies ran while one was open for 1% of the time, Pallas kernels for 7%

profile of v4, /device:TPU:1, one launch (start us, length us, event | category | flops | bytes accessed | tf_op | source)
XLA Modules:
  0.0 42.6 jit_solution(3918875332813637386)
XLA Ops:
  0.0 0.0 copy-start
  0.0 0.8 %pad_add_fusion = s32[148]{0:T(256)S(1)} fusion(s32[20]{0:T(128)} %param.6, s32[128]{0:T(128)} %param.7), kind=kLoop, calls=%fused_computation.2 | loop fusion | flops 148 | bytes 1184 | tf_op jit(solution)/shard_map/concatenate | solution.py:139
  0.8 7.4 %fourier.1.own = bf16[20,64,256]{2,1,0:T(8,128)(2,1)S(1)} custom-call(s32[256]{0:T(256)S(1)} %pad.4.numbers, s32[1,256]{1,0:T(1,128)S(1)} %bitcast.13, bf16[20,64,5136]{2,1,0:T(8,128)(2,1)} %bitcast.15), custom_call_target="tpu_custom_call" | custom-call | tf_op jit(solution)/shard_map/fourier/pallas_call | solution.py:140
  8.2 1.5 %collective-permute-start = (bf16[20,64,256]{2,1,0:T(8,128)(2,1)S(1)}, bf16[20,64,256]{2,1,0:T(8,128)(2,1)S(1)}, u32[]{:S(2)}, u32[]{:S(2)}) collective-permute-start(bf16[20,64,256]{2,1,0:T(8,128)(2,1)S(1)} %fourier.1.own), channel_id=1, source_target_pairs={{0,1},{1,0},{2,3},{3,2},{4,5},{5,4},{6,7},{7,6},{8,9},{9,8},{10,11... | collective-permute-start | bytes 1966088 | tf_op jit(solution)/shard_map/ppermute | solution.py:312
  9.7 0.0 copy-done
  9.7 0.5 %copy.6 = bf16[40,16,2,32]{3,2,1,0:T(2,128)(2,1)S(1)} copy(bf16[40,16,2,32]{0,3,1,2:T(8,128)(2,1)S(1)} %fusion) | data formatting | bytes 163840 | tf_op jit(solution)/shard_map/transpose | solution.py:314
  10.2 1.2 %fold.1 = (bf16[20,64,128]{2,1,0:T(8,128)(2,1)S(1)}, bf16[320,1280]{1,0:T(8,128)(2,1)S(1)}) custom-call(bf16[1280,32]{1,0:T(8,128)(2,1)S(1)} %bitcast.11, bf16[2,2,320,1280]{3,2,1,0:T(8,128)(2,1)} %table.3), custom_call_target="tpu_custom_call" | custom-call | flops 16777216 | bytes 4194304 | tf_op jit(solution)/shard_map/fold/pallas_call | solution.py:183
  11.4 0.0 collective-permute-done.other
  11.4 0.0 copy-start.1
  11.4 0.6 %mix.1 = bf16[2560,128]{1,0:T(8,128)(2,1)S(1)} custom-call(bf16[20,64,128]{2,1,0:T(8,128)(2,1)S(1)} %get-tuple-element.9.matrices, bf16[20,64,256]{2,1,0:T(8,128)(2,1)S(1)} %fourier.1.own, bf16[20,64,256]{2,1,0:T(8,128)(2,1)S(1)} %collective-permute-done.other), custom_call_target="tpu_custom_call" | custom-call | tf_op jit(solution)/shard_map/mix/pallas_call | solution.py:213
  12.0 24.9 %all_to_all.5 = bf16[64,40,128]{2,1,0:T(8,128)(2,1)S(1)} all-to-all(bf16[64,40,128]{2,1,0:T(8,128)(2,1)S(1)} %bitcast.9), channel_id=1, replica_groups=mesh['lat'=64,'lev'=2] {'lat'}, dimensions={0} | all-to-all | bytes 1310720 | tf_op jit(solution)/shard_map/all_to_all | solution.py:317
  36.9 1.8 %collective-permute-start.1 = (bf16[64,40,128]{2,1,0:T(8,128)(2,1)S(1)}, bf16[64,40,128]{2,1,0:T(8,128)(2,1)S(1)}, u32[]{:S(2)}, u32[]{:S(2)}) collective-permute-start(bf16[64,40,128]{2,1,0:T(8,128)(2,1)S(1)} %all_to_all.5), channel_id=1, source_target_pairs={{0,1},{1,0},{2,3},{3,2},{4,5},{5,4},{6,7},{7,6},{8,9},{9,8},{10,11... | collective-permute-start | bytes 1966088 | tf_op jit(solution)/shard_map/ppermute | solution.py:320
  38.8 1.7 %prepare.1 = (bf16[2,2,1280,128]{3,2,1,0:T(8,128)(2,1)S(1)}, bf16[3,320,1280]{2,1,0:T(8,128)(2,1)S(1)}) custom-call(bf16[2560,128]{1,0:T(8,128)(2,1)S(1)} %bitcast.10, bf16[2,2,320,1280]{3,2,1,0:T(8,128)(2,1)} %table.3), custom_call_target="tpu_custom_call" | custom-call | flops 167772160 | bytes 4194304 | tf_op jit(solution)/shard_map/prepare/pallas_call | solution.py:248
  40.5 0.0 collective-permute-done.1
  40.5 0.0 copy-done.1
  40.5 2.1 %legendre.1 = bf16[2,2,320,128]{3,2,1,0:T(8,128)(2,1)} custom-call(s32[1,128]{1,0:T(1,128)S(1)} %bitcast.14, bf16[2,2,1280,128]{3,2,1,0:T(8,128)(2,1)S(1)} %get-tuple-element.10.folded, bf16[2560,128]{1,0:T(8,128)(2,1)S(1)} %bitcast.12, bf16[320,1280]{1,0:T(8,128)(2,1)S(1)} %get-tuple-element.11.first_table, ...), custom_call_target="tpu_custom_call" | custom-call | tf_op jit(solution)/shard_map/legendre/pallas_call | solution.py:292
  (2 shorter events, 0.0 us)
Async XLA Ops:
  0.0 9.7 %copy-start = (f32[40,2,32,32]{0,3,2,1:T(8,128)S(1)}, f32[40,2,32,32]{0,3,2,1:T(8,128)}, u32[]{:S(2)}) copy-start(f32[40,2,32,32]{0,3,2,1:T(8,128)} %param.8) | copy-start | bytes 983044
  8.2 3.2 %collective-permute-start = (bf16[20,64,256]{2,1,0:T(8,128)(2,1)S(1)}, bf16[20,64,256]{2,1,0:T(8,128)(2,1)S(1)}, u32[]{:S(2)}, u32[]{:S(2)}) collective-permute-start(bf16[20,64,256]{2,1,0:T(8,128)(2,1)S(1)} %fourier.1.own), channel_id=1, source_target_pairs={{0,1},{1,0},{2,3},{3,2},{4,5},{5,4},{6,7},{7,6},{8,9},{9,8},{10,11... | collective-permute-start | bytes 1966088 | tf_op jit(solution)/shard_map/ppermute | solution.py:312
  11.4 29.1 %copy-start.1 = (s32[128]{0:T(128)S(1)}, s32[128]{0:T(128)}, u32[]{:S(2)}) copy-start(s32[128]{0:T(128)} %param.7) | copy-start | bytes 1540
  36.9 3.6 %collective-permute-start.1 = (bf16[64,40,128]{2,1,0:T(8,128)(2,1)S(1)}, bf16[64,40,128]{2,1,0:T(8,128)(2,1)S(1)}, u32[]{:S(2)}, u32[]{:S(2)}) collective-permute-start(bf16[64,40,128]{2,1,0:T(8,128)(2,1)S(1)} %all_to_all.5), channel_id=1, source_target_pairs={{0,1},{1,0},{2,3},{3,2},{4,5},{5,4},{6,7},{7,6},{8,9},{9,8},{10,11... | collective-permute-start | bytes 1966088 | tf_op jit(solution)/shard_map/ppermute | solution.py:320

commit v5 on v4

--- a/solution.py
+++ b/solution.py
@@ -9,8 +9,8 @@
 
 TRUNC = 1279
 BLOCK = 256
-GROUP = 4
-AHEAD = 8
+GROUPS = (4, 4, 4, 4, 2, 2)
+AHEAD = 16
 FOURIER_VMEM = 53 * 2**20
 FOLD_VMEM = 51 * 2**20
 PREPARE_VMEM = 48 * 2**20
@@ -107,31 +107,23 @@
             )
         out[p] = jnp.concatenate([real * scale, imag * scale], 1).astype(bf16)
 
-    def basis_step(t, carry):
-        for i in range(GROUP):
-            make_basis(t * GROUP + i)
-        return carry
-
-    lax.fori_loop(0, pairs // GROUP, basis_step, 0)
-
-    def group_step(t, carry):
-        @pl.when(t * GROUP + AHEAD < pairs)
-        def _():
-            for i in range(GROUP):
-                fetch(t * GROUP + AHEAD + i).start()
-
-        for i in range(GROUP):
-            fetch(t * GROUP + i).wait()
-        for i in range(GROUP):
-            p = t * GROUP + i
+    starts = [sum(GROUPS[:g]) for g in range(len(GROUPS))]
+    for p in range(pairs):
+        make_basis(p)
+    fetched = AHEAD
+    for begin, size in zip(starts, GROUPS):
+        group = range(begin, begin + size)
+        for p in range(fetched, min(pairs, begin + AHEAD + size)):
+            fetch(p).start()
+            fetched = p + 1
+        for p in group:
+            fetch(p).wait()
+        for p in group:
             first = jnp.minimum(counts[p] // BLOCK, blocks - 1) * BLOCK
             at = pl.ds(pl.multiple_of(first, BLOCK), BLOCK)
             values[p, :, at] = clear_beyond(values[p, :, at], first, counts[p])
-        for i in range(GROUP):
-            transform(t * GROUP + i, i)
-        return carry
-
-    lax.fori_loop(0, pairs // GROUP, group_step, 0)
+        for p in group:
+            transform(p, p - begin)
 
 
 def fourier(grouped, lat_counts, wave_table):
@@ -150,7 +142,7 @@
             pltpu.VMEM((pairs, rows, storage), bf16),
             pltpu.VMEM((pairs, BLOCK, 256), bf16),
             pltpu.VMEM((pairs, 24, 128), f32),
-            pltpu.VMEM((GROUP, rows, BLOCK), bf16),
+            pltpu.VMEM((max(GROUPS), rows, BLOCK), bf16),
             pltpu.SMEM((256,), jnp.int32),
             pltpu.SemaphoreType.DMA((pairs,)),
             pltpu.SemaphoreType.DMA,
@@ -264,7 +256,7 @@
     )(own, table)
 
 
-def legendre_kernel(waves, folded, other, first_table, second_table, out, rows, both):
+def legendre_kernel(waves, folded, other, first_table, second_table, out, rows, both, done, sems):
     slots, parities, degree_rows, _ = out.shape
     pairs = folded.shape[2]
     slab = lax.axis_index("lev")
@@ -276,6 +268,7 @@
         same, opposite = unfold(rows[pl.ds(s, pairs, stride=slots), :], 1 - slab)
         both[s, 1 - slab] = jnp.where(mine, folded[s, 1 - slab], same.astype(bf16))
         both[s, slab] = jnp.where(mine, folded[s, slab], opposite.astype(bf16))
+    stores = []
     for s in range(slots):
         here = iota((1, 128), 1) == owner * slots + s
         wave = jnp.sum(jnp.where(here, waves[...], 0), axis=1, keepdims=True)
@@ -283,7 +276,12 @@
             table = first_table[...] if s + q == 0 else second_table[s * parities + q - 1]
             summed = jnp.dot(table, both[s, q], preferred_element_type=f32)
             degree = wave + 2 * (slab * degree_rows + iota(summed.shape, 0)) + q
-            out[s, q] = jnp.where(degree <= TRUNC, summed, 0.0).astype(bf16)
+            done[s, q] = jnp.where(degree <= TRUNC, summed, 0.0).astype(bf16)
+            store = pltpu.make_async_copy(done.at[s, q], out.at[s, q], sems.at[s, q])
+            store.start()
+            stores.append(store)
+    for store in stores:
+        store.wait()
 
 
 def legendre_sum(wave_table, folded, other, first_table, second_table):
@@ -293,10 +291,12 @@
         legendre_kernel,
         out_shape=jax.ShapeDtypeStruct((slots, parities, degree_rows, 128), bf16),
         in_specs=[pl.BlockSpec(memory_space=pltpu.VMEM)] * 5,
-        out_specs=pl.BlockSpec(memory_space=pltpu.VMEM),
+        out_specs=pl.BlockSpec(memory_space=pl.ANY),
         scratch_shapes=[
             pltpu.VMEM((slots * pairs, 128), f32),
             pltpu.VMEM((slots, parities, pairs, 128), bf16),
+            pltpu.VMEM((slots, parities, degree_rows, 128), bf16),
+            pltpu.SemaphoreType.DMA((slots, parities)),
         ],
         compiler_params=pltpu.CompilerParams(vmem_limit_bytes=LEGENDRE_VMEM),
         name="legendre",

time: 42.8 us -> 42.8 us (level)
  no operation moved by 1% of the time
where the time goes in v5:
time: 42.8 us; the launch traced here: 42.6 us
  blocking collectives  24.9 us (58%)
  Pallas kernels  13 us (30%)
  starting transfers between devices  3.32 us (8%)
  other arithmetic  0.77 us (2%)
  local copies, waits for them, and re-layouts  0.55 us (1%)
    all_to_all x1, blocking collectives, on_device(): lax.all_to_all(send.reshape(64, 40, 128), 'lat', split_axis=0, concat_axi...  24.9 us
    pallas_call x1, Pallas kernels, fourier(): pl.pallas_call(fourier_kernel, out_shape=jax.ShapeDtypeStruct((pairs, row...  7.43 us
    pallas_call x1, Pallas kernels, legendre_sum(): pl.pallas_call(legendre_kernel, out_shape=jax.ShapeDtypeStruct((slots, pa...  2.04 us
    ppermute x1, starting transfers between devices, on_device(): rest = lax.ppermute(slab, 'lev', swap)  1.82 us
    pallas_call x1, Pallas kernels, prepare(): pl.pallas_call(prepare_kernel, out_shape=[jax.ShapeDtypeStruct((slots, pa...  1.72 us
    ppermute x1, starting transfers between devices, on_device(): other = lax.ppermute(own, 'lev', swap)  1.5 us
    pallas_call x1, Pallas kernels, fold_matrices(): pl.pallas_call(fold_kernel, out_shape=[jax.ShapeDtypeStruct((inverses.sha...  1.16 us
  transfers between devices with their start and end apart: 2, of which 0 were waited for; matrix products, arithmetic and copies ran while one was open for 1% of the time, Pallas kernels for 7%

profile of v5, /device:TPU:1, one launch (start us, length us, event | category | flops | bytes accessed | tf_op | source)
XLA Modules:
  0.0 42.6 jit_solution(5045040331179813578)
XLA Ops:
  0.0 0.0 copy-start
  0.0 0.8 %pad_add_fusion = s32[148]{0:T(256)S(1)} fusion(s32[20]{0:T(128)} %param.6, s32[128]{0:T(128)} %param.7), kind=kLoop, calls=%fused_computation.2 | loop fusion | flops 148 | bytes 1184 | tf_op jit(solution)/shard_map/concatenate | solution.py:131
  0.8 7.4 %fourier.1.own = bf16[20,64,256]{2,1,0:T(8,128)(2,1)S(1)} custom-call(s32[256]{0:T(256)S(1)} %pad.4.numbers, s32[1,256]{1,0:T(1,128)S(1)} %bitcast.13, bf16[20,64,5136]{2,1,0:T(8,128)(2,1)} %bitcast.15), custom_call_target="tpu_custom_call" | custom-call | tf_op jit(solution)/shard_map/fourier/pallas_call | solution.py:132
  8.2 1.5 %collective-permute-start = (bf16[20,64,256]{2,1,0:T(8,128)(2,1)S(1)}, bf16[20,64,256]{2,1,0:T(8,128)(2,1)S(1)}, u32[]{:S(2)}, u32[]{:S(2)}) collective-permute-start(bf16[20,64,256]{2,1,0:T(8,128)(2,1)S(1)} %fourier.1.own), channel_id=1, source_target_pairs={{0,1},{1,0},{2,3},{3,2},{4,5},{5,4},{6,7},{7,6},{8,9},{9,8},{10,11... | collective-permute-start | bytes 1966088 | tf_op jit(solution)/shard_map/ppermute | solution.py:312
  9.7 0.0 copy-done
  9.8 0.5 %copy.6 = bf16[40,16,2,32]{3,2,1,0:T(2,128)(2,1)S(1)} copy(bf16[40,16,2,32]{0,3,1,2:T(8,128)(2,1)S(1)} %fusion) | data formatting | bytes 163840 | tf_op jit(solution)/shard_map/transpose | solution.py:314
  10.3 1.2 %fold.1 = (bf16[20,64,128]{2,1,0:T(8,128)(2,1)S(1)}, bf16[320,1280]{1,0:T(8,128)(2,1)S(1)}) custom-call(bf16[1280,32]{1,0:T(8,128)(2,1)S(1)} %bitcast.11, bf16[2,2,320,1280]{3,2,1,0:T(8,128)(2,1)} %table.3), custom_call_target="tpu_custom_call" | custom-call | flops 16777216 | bytes 4194304 | tf_op jit(solution)/shard_map/fold/pallas_call | solution.py:175
  11.4 0.0 collective-permute-done.other
  11.4 0.0 copy-start.1
  11.5 0.6 %mix.1 = bf16[2560,128]{1,0:T(8,128)(2,1)S(1)} custom-call(bf16[20,64,128]{2,1,0:T(8,128)(2,1)S(1)} %get-tuple-element.9.matrices, bf16[20,64,256]{2,1,0:T(8,128)(2,1)S(1)} %fourier.1.own, bf16[20,64,256]{2,1,0:T(8,128)(2,1)S(1)} %collective-permute-done.other), custom_call_target="tpu_custom_call" | custom-call | tf_op jit(solution)/shard_map/mix/pallas_call | solution.py:205
  12.1 24.9 %all_to_all.5 = bf16[64,40,128]{2,1,0:T(8,128)(2,1)S(1)} all-to-all(bf16[64,40,128]{2,1,0:T(8,128)(2,1)S(1)} %bitcast.9), channel_id=1, replica_groups=mesh['lat'=64,'lev'=2] {'lat'}, dimensions={0} | all-to-all | bytes 1310720 | tf_op jit(solution)/shard_map/all_to_all | solution.py:317
  37.0 1.8 %collective-permute-start.1 = (bf16[64,40,128]{2,1,0:T(8,128)(2,1)S(1)}, bf16[64,40,128]{2,1,0:T(8,128)(2,1)S(1)}, u32[]{:S(2)}, u32[]{:S(2)}) collective-permute-start(bf16[64,40,128]{2,1,0:T(8,128)(2,1)S(1)} %all_to_all.5), channel_id=1, source_target_pairs={{0,1},{1,0},{2,3},{3,2},{4,5},{5,4},{6,7},{7,6},{8,9},{9,8},{10,11... | collective-permute-start | bytes 1966088 | tf_op jit(solution)/shard_map/ppermute | solution.py:320
  38.8 1.7 %prepare.1 = (bf16[2,2,1280,128]{3,2,1,0:T(8,128)(2,1)S(1)}, bf16[3,320,1280]{2,1,0:T(8,128)(2,1)S(1)}) custom-call(bf16[2560,128]{1,0:T(8,128)(2,1)S(1)} %bitcast.10, bf16[2,2,320,1280]{3,2,1,0:T(8,128)(2,1)} %table.3), custom_call_target="tpu_custom_call" | custom-call | flops 167772160 | bytes 4194304 | tf_op jit(solution)/shard_map/prepare/pallas_call | solution.py:240
  40.6 0.0 collective-permute-done.1
  40.6 0.0 copy-done.1
  40.6 2.0 %legendre.1 = bf16[2,2,320,128]{3,2,1,0:T(8,128)(2,1)} custom-call(s32[1,128]{1,0:T(1,128)S(1)} %bitcast.14, bf16[2,2,1280,128]{3,2,1,0:T(8,128)(2,1)S(1)} %get-tuple-element.10.folded, bf16[2560,128]{1,0:T(8,128)(2,1)S(1)} %bitcast.12, bf16[320,1280]{1,0:T(8,128)(2,1)S(1)} %get-tuple-element.11.first_table, ...), custom_call_target="tpu_custom_call" | custom-call | tf_op jit(solution)/shard_map/legendre/pallas_call | solution.py:290
  (2 shorter events, 0.0 us)
Async XLA Ops:
  0.0 9.7 %copy-start = (f32[40,2,32,32]{0,3,2,1:T(8,128)S(1)}, f32[40,2,32,32]{0,3,2,1:T(8,128)}, u32[]{:S(2)}) copy-start(f32[40,2,32,32]{0,3,2,1:T(8,128)} %param.8) | copy-start | bytes 983044
  8.2 3.2 %collective-permute-start = (bf16[20,64,256]{2,1,0:T(8,128)(2,1)S(1)}, bf16[20,64,256]{2,1,0:T(8,128)(2,1)S(1)}, u32[]{:S(2)}, u32[]{:S(2)}) collective-permute-start(bf16[20,64,256]{2,1,0:T(8,128)(2,1)S(1)} %fourier.1.own), channel_id=1, source_target_pairs={{0,1},{1,0},{2,3},{3,2},{4,5},{5,4},{6,7},{7,6},{8,9},{9,8},{10,11... | collective-permute-start | bytes 1966088 | tf_op jit(solution)/shard_map/ppermute | solution.py:312
  11.4 29.1 %copy-start.1 = (s32[128]{0:T(128)S(1)}, s32[128]{0:T(128)}, u32[]{:S(2)}) copy-start(s32[128]{0:T(128)} %param.7) | copy-start | bytes 1540
  37.0 3.6 %collective-permute-start.1 = (bf16[64,40,128]{2,1,0:T(8,128)(2,1)S(1)}, bf16[64,40,128]{2,1,0:T(8,128)(2,1)S(1)}, u32[]{:S(2)}, u32[]{:S(2)}) collective-permute-start(bf16[64,40,128]{2,1,0:T(8,128)(2,1)S(1)} %all_to_all.5), channel_id=1, source_target_pairs={{0,1},{1,0},{2,3},{3,2},{4,5},{5,4},{6,7},{7,6},{8,9},{9,8},{10,11... | collective-permute-start | bytes 1966088 | tf_op jit(solution)/shard_map/ppermute | solution.py:320
